TPU v7x, 256 devices: a whole 4x4x8 slice. The times are simulated.
256 devices in a mesh: lat: 8 (over z), lon: 8 (over x, core), mem: 4 (over y).
Axes of the slice: x: 4, y: 4, z: 8, core: 2. Of those that a mesh axis runs over, the one named last changes fastest.
Arguments:
- latent: bfloat16 [4, 96, 1024, 1024], P('mem', 'lat', 'lon'), may hold values from -6 to 6
- norm_gain: float32 [1024], replicated, may hold values from 0.1 to 1.9
- hidden_weight: bfloat16 [1024, 1024], replicated, may hold values from -0.1875 to 0.1875
- hidden_bias: float32 [1024], replicated, may hold values from -3 to 3
- output_weight: bfloat16 [1024, 80], replicated, may hold values from -0.1875 to 0.1875
- flux_table: float32 [3, 80], replicated, may hold values from -4 to 4
- target: float32 [4, 96], P('mem', 'lat'), may hold values from -8 to 8
- land_sea: int32 [96, 1024], P('lat', 'lon'), may hold values from 0 to 2
- band_index: int32 [96], P('lat'), may hold values from 1 to 719, as said below
Outputs:
- grad_latent: bfloat16 [4, 96, 1024, 1024], P('mem', 'lat', 'lon')
- grad_hidden_weight: float32 [1024, 1024], P('mem')
- grad_output_weight: float32 [1024, 80], replicated
- grad_gain: float32 [1024], replicated
- grad_hidden_bias: float32 [1024], replicated
Inputs may be any that keep to these rules, and one draw needn't show every extreme that they name: `band_index`: strictly increasing along the rows; the first row is band 1 and the last band 719.
All inputs are finite; a program needn't handle non-finite values.
Results may differ from a plain program's by a relative error of at most 0.006.
Values sent between devices are 32-bit elements; how exact they have to be, the bound alone decides.
A program may use at most 128 MiB of HBM per device.

v0:
```python
import jax
import jax.numpy as jnp
from jax import lax
from jax.sharding import PartitionSpec as P


def prefix(array, axis, combine, identity, reverse):
    count, here = (lax.axis_size(axis), lax.axis_index(axis))
    everything = lax.all_gather(array, axis)
    start = jnp.broadcast_to(jnp.asarray(identity, array.dtype), array.shape)

    def step(k, before):
        at = count - 1 - k if reverse else k
        reached = at > here if reverse else at < here
        new = combine(before, everything[at])
        return jnp.where(reached, new, before)

    return lax.fori_loop(0, count, step, start)


def contract_cells(left, right):
    return lax.dot_general(
        left, right, (((0,), (0,)), ((), ())), preferred_element_type=jnp.float32
    )


def decode(flat_cells, norm_gain, hidden_weight, hidden_bias, output_weight):
    features = flat_cells.astype(jnp.float32)
    inv_rms = lax.rsqrt(jnp.mean(features * features, axis=-1, keepdims=True) + 1e-05)
    normed = (features * inv_rms * norm_gain).astype(jnp.bfloat16)
    preact = jnp.dot(normed, hidden_weight, preferred_element_type=jnp.float32) + hidden_bias
    active = jax.nn.silu(preact).astype(jnp.bfloat16)
    decoded = jnp.dot(active, output_weight, preferred_element_type=jnp.float32)
    return (features, inv_rms, normed, preact, active, decoded)


def surface_table(cell_types, flux_table):
    onehot = (cell_types[:, None] == jnp.arange(3, dtype=jnp.int32)[None, :]).astype(jnp.float32)
    return jnp.dot(onehot, flux_table, precision=lax.Precision.HIGHEST)


def add_terms(earlier, later):
    return earlier + later


def on_device(
    latent,
    norm_gain,
    hidden_weight,
    hidden_bias,
    output_weight,
    flux_table,
    target,
    land_sea,
    band_index,
):
    members, rows_here, cols_here, width = latent.shape
    flat_cells = latent.reshape(-1, width)
    cell_types = land_sea[None].reshape(-1)
    features, inv_rms, normed, preact, active, decoded = decode(
        flat_cells, norm_gain, hidden_weight, hidden_bias, output_weight
    )
    table = surface_table(cell_types, flux_table)
    row_partial = jnp.sum((decoded * table).reshape(members, rows_here, cols_here, -1), axis=(2, 3))
    row_total = lax.psum(row_partial, "lon")
    zonal = row_total / (cols_here * lax.axis_size("lon"))
    coslat = jnp.cos(jnp.pi * (band_index.astype(jnp.float32) / 720.0 - 0.5))
    weighted = coslat[None, :] * zonal
    total_rows = rows_here * lax.axis_size("lat")
    local_north = jnp.cumsum(weighted, axis=1)
    below = prefix(local_north[:, -1], "lat", add_terms, jnp.zeros((members,), jnp.float32), False)
    misfit = local_north + below[:, None] - target
    local_south = lax.cumsum(misfit, axis=1, reverse=True)
    above = prefix(local_south[:, 0], "lat", add_terms, jnp.zeros((members,), jnp.float32), True)
    southward = local_south + above[:, None]
    flux_grad = coslat[None, :] * southward / total_rows
    cell_grad = jnp.broadcast_to(flux_grad[:, :, None], (members, rows_here, cols_here)).reshape(-1)
    decoded_grad = (cell_grad[:, None] * table).astype(jnp.bfloat16)
    grad_out = contract_cells(active, decoded_grad)
    active_grad = lax.dot_general(
        decoded_grad, output_weight, (((1,), (1,)), ((), ())), preferred_element_type=jnp.float32
    )
    sigma = jax.nn.sigmoid(preact)
    preact_grad = (active_grad * sigma * (1.0 + preact * (1.0 - sigma))).astype(jnp.bfloat16)
    grad_bias = jnp.sum(preact_grad.astype(jnp.float32), axis=0)
    normed_grad = lax.dot_general(
        preact_grad, hidden_weight, (((1,), (1,)), ((), ())), preferred_element_type=jnp.float32
    )
    grad_gain = jnp.sum(normed_grad * features * inv_rms, axis=0)
    scaled = normed_grad * norm_gain
    grad_cells = inv_rms * scaled - features * inv_rms**3 * jnp.mean(
        scaled * features, axis=-1, keepdims=True
    )
    grad_latent = grad_cells.astype(jnp.bfloat16).reshape(members, rows_here, cols_here, width)
    share_rows = width // lax.axis_size("mem")
    grad_hidden = contract_cells(normed, preact_grad)
    summed = lax.psum((grad_hidden, grad_out, grad_gain, grad_bias), ("lat", "lon", "mem"))
    hidden_share = lax.dynamic_slice_in_dim(
        summed[0], lax.axis_index("mem") * share_rows, share_rows, 0
    )
    out_total, gain_total, bias_total = (summed[1], summed[2], summed[3])
    return (grad_latent, hidden_share, out_total, gain_total, bias_total)


def solution(mesh):
    return jax.shard_map(
        on_device,
        mesh=mesh,
        in_specs=(
            P("mem", "lat", "lon", None),
            P(),
            P(),
            P(),
            P(),
            P(),
            P("mem", "lat"),
            P("lat", "lon"),
            P("lat"),
        ),
        out_specs=(P("mem", "lat", "lon", None), P("mem", None), P(), P(), P()),
        check_vma=False,
    )
```

profile of v0, /device:TPU:1, one launch (start us, length us, event | category | flops | bytes accessed | tf_op | source)
XLA Modules:
  0.0 390.5 jit_solution(11338630799477085856)
XLA Ops:
  7.2 0.0 copy-start
  7.2 0.0 copy-start.8
  7.2 0.0 all-reduce.6.cloned.1.call-start
  7.2 2.7 fusion
  10.0 2.0 fusion.10
  11.9 2.7 fusion.2
  14.6 0.0 copy-done
  14.6 0.0 copy-done.8
  14.6 0.0 copy-start.2
  14.6 0.0 copy-start.4
  14.7 0.0 copy-start.7
  14.7 0.0 copy-start.9
  14.7 6.0 %multiply_convert_fusion.1 = (bf16[1536,1024]{1,0:T(8,128)(2,1)S(1)}, f32[1536,1024]{1,0:T(8,128)}) fusion(f32[1024]{0:T(1024)S(1)} %copy-done.8, bf16[1536,1024]{1,0:T(8,128)(2,1)S(1)} %fusion.2, bf16[1024,1024]{1,0:T(8,128)(2,1)S(1)} %copy-done), kind=kOutput, calls=%fused_computation.18 | convolution fusion | flops 3230662656 | bytes 14684160 | tf_op jit(solution)/shard_map/dot_general | solution.py:31
  20.7 0.0 copy-done.2
  20.7 0.0 copy-start.1
  20.7 1.7 copy-done.1
  22.3 0.0 copy-done.4
  22.3 1.1 fusion.9
  23.4 0.1 bitcast_reduce_fusion
  23.5 15.0 %psum.35 = f32[1,12]{1,0:T(1,128)S(1)} all-reduce(f32[1,12]{1,0:T(1,128)S(1)} %bitcast.73), channel_id=1, replica_groups=mesh['lat'=8,'lon'=8,'mem'=4] {'lon'}, use_global_device_ids=true, to_apply=%region_3.4 | all-reduce | flops 12 | bytes 96 | tf_op jit(solution)/shard_map/psum | solution.py:65
  38.5 0.0 copy-done.7
  38.6 0.2 reduce_window_sum.21
  38.8 0.6 slice.6
  39.4 0.0 copy-done.9
  39.4 0.6 dynamic-slice
  40.0 1.3 bitcast_dynamic-update-slice_fusion.1
  41.3 14.5 %all-reduce = f32[8]{0:T(128)S(1)} all-reduce(f32[8]{0:T(128)S(1)} %bitcast_dynamic-update-slice_fusion.1), channel_id=1, replica_groups=mesh['lat'=8,'lon'=8,'mem'=4] {'lat'}, use_global_device_ids=true, to_apply=%add | all-reduce | flops 8 | bytes 64
  55.8 10.5 %while.28 = (s32[]{:T(128)}, f32[1]{0:T(128)}, s32[]{:T(128)}, f32[8,1]{0,1:T(1,128)S(1)}, s32[]{:T(128)}) while((s32[]{:T(128)}, f32[1]{0:T(128)}, s32[]{:T(128)}, f32[8,1]{0,1:T(1,128)S(1)}, s32[]{:T(128)}) %tuple.78), condition=%wide.region_6.7_spmd, body=%wide.region_5.6_spmd.sunk | while | flops 5 | bytes 115 | solution.py:18
  55.8 0.7 constant_dynamic-slice_fusion.5
  57.1 0.7 constant_dynamic-slice_fusion.5
  58.5 0.7 constant_dynamic-slice_fusion.5
  59.8 0.7 constant_dynamic-slice_fusion.5
  61.1 0.7 constant_dynamic-slice_fusion.5
  62.4 0.7 constant_dynamic-slice_fusion.5
  63.7 0.7 constant_dynamic-slice_fusion.5
  65.0 0.7 constant_dynamic-slice_fusion.5
  66.4 0.0 copy-done.6
  66.4 0.2 reduce_window_sum.22
  66.6 0.7 bitcast_dynamic-update-slice_fusion
  67.2 10.7 %all-reduce.1 = f32[8]{0:T(128)S(1)} all-reduce(f32[8]{0:T(128)S(1)} %bitcast_dynamic-update-slice_fusion), channel_id=1, replica_groups=mesh['lat'=8,'lon'=8,'mem'=4] {'lat'}, use_global_device_ids=true, to_apply=%add.1 | all-reduce | flops 8 | bytes 64
  77.9 10.4 %while.29 = (s32[]{:T(128)}, f32[1]{0:T(128)}, s32[]{:T(128)}, f32[8,1]{0,1:T(1,128)S(1)}, s32[]{:T(128)}, /*index=5*/s32[]{:T(128)}, s32[]{:T(128)}, s32[]{:T(128)}) while((s32[]{:T(128)}, f32[1]{0:T(128)}, s32[]{:T(128)}, f32[8,1]{0,1:T(1,128)S(1)}, s32[]{:T(128)}, /*index=5*/s32[]{:T(128)}, s32[]{:T(128)}, s32[]{:T(128)}) %tuple.77), condition=%wide.region_9.10_spmd, body=%wide.region_8.9_spmd.sunk | while | flops 9 | bytes 185 | solution.py:18
  77.9 0.6 constant_dynamic-slice_fusion.6
  79.2 0.6 constant_dynamic-slice_fusion.6
  80.5 0.6 constant_dynamic-slice_fusion.6
  81.8 0.6 constant_dynamic-slice_fusion.6
  83.1 0.6 constant_dynamic-slice_fusion.6
  84.4 0.6 constant_dynamic-slice_fusion.6
  85.7 0.6 constant_dynamic-slice_fusion.6
  87.0 0.6 constant_dynamic-slice_fusion.6
  88.3 0.1 broadcast_bitcast_fusion
  88.4 3.3 fusion.12
  91.7 5.1 %convert_reduce_fusion = (f32[1024]{0:T(1024)S(1)}, bf16[1536,1024]{1,0:T(8,128)(2,1)S(1)}) fusion(f32[1536,1024]{1,0:T(8,128)} %get-tuple-element.219, f32[1024]{0:T(1024)S(1)} %copy-done.8, bf16[1024,80]{0,1:T(8,128)(2,1)S(1)} %copy-done.4, f32[1536,80]{0,1:T(8,128)S(1)} %fusion.10, f32[1536]{0:T(1024)S(1)} %broadcast_bitcast_fusion), kind=kOutput, calls=%fused_computation.16 | convolution fusion | flops 270777344 | bytes 10106880 | tf_op jit(solution)/shard_map/dot_general | solution.py:80
  96.8 0.0 copy-start.10
  96.8 1.7 copy-done.10
  98.4 0.0 copy-done.3
  98.4 5.0 %fusion.14 = f32[1024,1024]{1,0:T(8,128)} fusion(bf16[1536,1024]{1,0:T(8,128)(2,1)S(1)} %copy-done.3, bf16[1536,1024]{1,0:T(8,128)(2,1)S(1)} %get-tuple-element.222), kind=kOutput, calls=%fused_computation.40 | convolution fusion | flops 3221225472 | bytes 10485760 | tf_op jit(solution)/shard_map/dot_general | solution.py:22
  103.5 0.0 all-reduce.6.cloned.1.call-update
  103.5 0.0 copy-done.5
  103.5 8.9 %fusion.8 = (f32[1024]{0:T(1024)S(1)}, f32[1536]{0:T(1024)S(1)}, f32[1536,1024]{1,0:T(8,128)}) fusion(bf16[1,12,128,1024]{3,2,1,0:T(8,128)(2,1)} %param.13, f32[1536]{0:T(1024)S(1)} %rsqrt_bitcast_fusion, f32[1024]{0:T(1024)S(1)} %copy-done.5, bf16[1536,1024]{1,0:T(8,128)(2,1)} %copy-done.10, bf16[1024,1024]{1,0:T(8,128)(2,1)S(1)} %copy-done), kind=kOutput, calls=%fused_computation.15 | convolution fusion | flops 3232232960 | bytes 14700544 | tf_op jit(solution)/shard_map/dot_general | solution.py:86
  112.4 85.0 %all-reduce.2 = (f32[1024]{0:T(1024)}, f32[1024]{0:T(1024)}) all-reduce(f32[1024]{0:T(1024)S(1)} %get-tuple-element.196, f32[1024]{0:T(1024)S(1)} %get-tuple-element.221), channel_id=1, replica_groups=mesh['lat'=8,'lon'=8,'mem'=4] {'lat','lon','mem'}, use_global_device_ids=true, to_apply=%region_14.15 | all-reduce | flops 2048 | bytes 16384 | tf_op jit(solution)/shard_map/psum | solution.py:97
  197.4 5.7 %fusion.5 = bf16[1536,1024]{1,0:T(8,128)(2,1)} fusion(bf16[1,12,128,1024]{3,2,1,0:T(8,128)(2,1)} %param.13, f32[1536,1024]{1,0:T(8,128)} %get-tuple-element.220, f32[1536]{0:T(1024)S(1)} %broadcast_multiply_fusion, f32[1536]{0:T(1024)S(1)} %multiply_multiply_fusion, f32[1024]{0:T(1024)S(1)} %copy-done.5, f32[1536]{0:T(1024)S(1)} %rsqrt_bitcast_fusion), kind=kLoop, calls=%fused_computation.12 | loop fusion | flops 11010048 | bytes 12605440 | tf_op jit(solution)/shard_map/convert_element_type | solution.py:94
  203.1 176.5 %all-reduce.6.cloned.1.call-done = (f32[1024,1024]{1,0:T(8,128)}, f32[1024,80]{0,1:T(8,128)}) async-done(((f32[1024,1024]{1,0:T(8,128)}, f32[1024,80]{0,1:T(8,128)}), (f32[1024,1024]{1,0:T(8,128)}, f32[1024,80]{0,1:T(8,128)})) %all-reduce.6.cloned.1.call-update) | async-done | bytes 4522000 | tf_op jit(solution)/shard_map/psum | solution.py:97
  379.6 2.3 constant_dynamic-slice_fusion.2
  382.0 1.7 copy.34
  (11 shorter events, 0.1 us)
Async XLA Ops:
  7.2 7.4 %copy-start = (bf16[1024,1024]{1,0:T(8,128)(2,1)S(1)}, bf16[1024,1024]{1,0:T(8,128)(2,1)}, u32[]{:S(2)}) copy-start(bf16[1024,1024]{1,0:T(8,128)(2,1)} %param.15) | copy-start | bytes 6291460
  7.2 7.4 %copy-start.8 = (f32[1024]{0:T(1024)S(1)}, f32[1024]{0:T(1024)}, u32[]{:S(2)}) copy-start(f32[1024]{0:T(1024)} %param.16) | copy-start | bytes 12292
  7.2 372.5 %all-reduce.6.cloned.1.call-start = ((), (), s32[]{:S(2)}) async-start(), calls=%async_computation | async-start | bytes 9043968 | tf_op jit(solution)/shard_map/psum | solution.py:97
  14.6 6.0 %copy-start.2 = (bf16[1536,1024]{1,0:T(8,128)(2,1)}, bf16[1536,1024]{1,0:T(8,128)(2,1)S(1)}, u32[]{:S(2)}) copy-start(bf16[1536,1024]{1,0:T(8,128)(2,1)S(1)} %fusion.2) | copy-start | bytes 9437188
  14.6 7.7 %copy-start.4 = (bf16[1024,80]{0,1:T(8,128)(2,1)S(1)}, bf16[1024,80]{0,1:T(8,128)(2,1)}, u32[]{:S(2)}) copy-start(bf16[1024,80]{0,1:T(8,128)(2,1)} %param.17) | copy-start | bytes 491524
  14.7 23.9 %copy-start.7 = (s32[12]{0:T(128)S(1)}, s32[12]{0:T(128)}, u32[]{:S(2)}) copy-start(s32[12]{0:T(128)} %param.21) | copy-start | bytes 148
  14.7 24.7 %copy-start.9 = (u32[256]{0:T(256)S(1)}, u32[256]{0:T(256)}, u32[]{:S(2)}) copy-start(u32[256]{0:T(256)} %constant.118) | copy-start | bytes 3076
  20.7 1.7 copy-start.1
  20.7 45.7 %copy-start.6 = (f32[1,12]{1,0:T(1,128)S(1)}, f32[1,12]{1,0:T(1,128)}, u32[]{:S(2)}) copy-start(f32[1,12]{1,0:T(1,128)} %param.19) | copy-start | bytes 148
  91.7 6.7 %copy-start.3 = (bf16[1536,1024]{1,0:T(8,128)(2,1)S(1)}, bf16[1536,1024]{1,0:T(8,128)(2,1)}, u32[]{:S(2)}) copy-start(bf16[1536,1024]{1,0:T(8,128)(2,1)} %copy-done.2) | copy-start | bytes 9437188
  96.8 1.7 copy-start.10
  98.4 5.1 %copy-start.5 = (f32[1024]{0:T(1024)S(1)}, f32[1024]{0:T(1024)}, u32[]{:S(2)}) copy-start(f32[1024]{0:T(1024)} %param.14) | copy-start | bytes 12292
Sparse Core Ops, SparseCore 0:
  103.6 275.9 all-reduce.5
where the time goes:
time: 392 us; the launch traced here: 391 us
  waiting for transfers between devices  177 us (45%)
  blocking collectives  125 us (32%)
  matrix products  31.3 us (8%)
  local copies, waits for them, and re-layouts  20.9 us (5%)
  between operations  14.2 us (4%)
  other arithmetic  11.7 us (3%)
  loops' own time  10.6 us (3%)
    psum x1, waiting for transfers between devices, on_device(): lax.psum((grad_hidden, grad_out, grad_gain, grad_bias), ('lat', 'lon', 'm...  177 us
    psum x1, blocking collectives, on_device(): lax.psum((grad_hidden, grad_out, grad_gain, grad_bias), ('lat', 'lon', 'm...  85 us
    unnamed x2, blocking collectives  25.2 us
    psum x1, blocking collectives, on_device(): row_total = lax.psum(row_partial, 'lon')  15 us
    another operation x2, loops' own time, prefix(): return lax.fori_loop(0, count, step, start)  10.6 us
    dynamic_slice x16, local copies, waits for them, and re-layouts, step(): new = combine(before, everything[at])  10.3 us
    dot_general x1, matrix products, on_device(): lax.dot_general(preact_grad, hidden_weight, (((1,), (1,)), ((), ())), pre...  8.9 us
    dot_general x2, matrix products, contract_cells(): lax.dot_general(left, right, (((0,), (0,)), ((), ())), preferred_element_...  8.31 us
  transfers between devices with their start and end apart: 1, of which 1 were waited for; matrix products, arithmetic and copies ran while one was open for 4% of the time, Pallas kernels for 0%

commit v1 on v0

v1 whole, which is shorter than its diff:
```python
import functools
import math

import jax
import jax.numpy as jnp
from jax import lax
from jax.experimental import pallas as pl
from jax.experimental.pallas import tpu as pltpu
from jax.sharding import PartitionSpec as P

MESH = pl.DeviceIdType.MESH
F32 = jnp.float32
BF16 = jnp.bfloat16
HIGH = lax.Precision.HIGHEST

CELLS = 1536
ROWS = 12
COLS = 128
D = 1024
CHUNK = 256
NCHUNK = CELLS // CHUNK
LANES = 128
TILES = D // LANES
NX, NY, NZ, NLON = 4, 4, 8, 8


def remote(src, dst, send_sem, recv_sem, **where):
    return pltpu.make_async_remote_copy(
        src_ref=src,
        dst_ref=dst,
        send_sem=send_sem,
        recv_sem=recv_sem,
        device_id=where,
        device_id_type=MESH,
    )


def kernel(
    lat_hbm, gain_ref, w1_hbm, bias_ref, w2_ref, table_ref, target_ref, types_ref, band_ref,
    outlat_hbm, outhid_hbm, outw_ref, outgain_ref, outbias_ref,
    x_ref, w1_ref, n_ref, nt_ref, v_ref, u_ref, inv_ref, coef_ref, tcol_ref, square_ref,
    q_ref, tab_ref, s_ref, b_ref, fb_ref, gacc_ref, stage_ref,
    mine_ref, ex1_ref, line_ref, ex2_ref,
    give_ref, take_ref, own_ref, pass_ref, plain_ref, agg_ref, part_ref, cross_ref, piece_ref, depth_ref,
    hid_ref, sm_ref, sm1_ref, t1_ref, sm2_ref, t2_ref, sm3_ref, smo_ref,
    xsem, wsem, osem, hsem,
    ex1_s, ex1_r, ex2_s, ex2_r, core_s, core_r, r4_s, r4_r, cross_s, cross_r, depth_s, depth_r,
    agz_s, agz_r, agx_s, agx_r, agc_s, agc_r, sm1_s, sm1_r, sm2_s, sm2_r, sm3_s, sm3_r, sm4_s, sm4_r,
):
    z = lax.axis_index("lat")
    lon = lax.axis_index("lon")
    y = lax.axis_index("mem")
    x = lon // 2
    core = lon % 2

    def lon_at(step):
        return lax.rem(x + step, NX) * 2 + core

    def chunk_rows(i):
        return pl.ds(i * CHUNK, CHUNK)

    loads = [pltpu.make_async_copy(lat_hbm.at[chunk_rows(i)], x_ref.at[chunk_rows(i)], xsem.at[i]) for i in range(NCHUNK)]
    wload = pltpu.make_async_copy(w1_hbm, w1_ref, wsem)
    loads[0].start()
    wload.start()
    for i in range(1, NCHUNK):
        loads[i].start()

    barrier = pltpu.get_barrier_semaphore()
    for k in range(1, NLON):
        pl.semaphore_signal(barrier, inc=1, device_id={"lon": lax.rem(lon + k, NLON)}, device_id_type=MESH)
    for k in range(1, NZ):
        pl.semaphore_signal(barrier, inc=1, device_id={"lat": lax.rem(z + k, NZ)}, device_id_type=MESH)
    for k in range(1, NY):
        pl.semaphore_signal(barrier, inc=1, device_id={"mem": lax.rem(y + k, NY)}, device_id_type=MESH)

    tab_ref[...] = jnp.zeros_like(tab_ref)
    tab_ref[0:3, :] = table_ref[...]
    table = tab_ref[...]
    high = table.astype(BF16)
    rest = table - high.astype(F32)
    middle = rest.astype(BF16)
    w2 = w2_ref[...]
    dims = (((1,), (1,)), ((), ()))
    q_ref[...] = lax.dot_general(high, w2, dims, preferred_element_type=F32) + lax.dot_general(
        middle, w2, dims, preferred_element_type=F32
    )
    square_ref[...] = jnp.zeros_like(square_ref)
    square_ref[0:ROWS, :] = types_ref[...].astype(F32)
    turned = square_ref[...].T
    for r in range(ROWS):
        tcol_ref[r * COLS : (r + 1) * COLS, :] = jnp.broadcast_to(turned[:, r : r + 1], (COLS, LANES))

    gain = gain_ref[...]
    bias = bias_ref[...]

    def normalise(i):
        rows = chunk_rows(i)
        loads[i].wait()
        xf = x_ref[rows, :].astype(F32)
        inv = lax.rsqrt(jnp.mean(xf * xf, axis=-1, keepdims=True) + 1e-05)
        inv_ref[rows, :] = jnp.broadcast_to(inv, (CHUNK, LANES))
        n_ref[rows, :] = (xf * inv * gain).astype(BF16)

    def first_dot(i):
        rows = chunk_rows(i)
        v_ref[rows, :] = jnp.dot(n_ref[rows, :], w1_ref[...], preferred_element_type=F32)

    kind = lax.broadcasted_iota(jnp.int32, (16, COLS), 0)

    def activate(i):
        rows = chunk_rows(i)
        p = v_ref[rows, :] + bias
        act = (p * (0.5 * jnp.tanh(0.5 * p) + 0.5)).astype(BF16)
        left = kind == types_ref[2 * i : 2 * i + 1, :]
        right = (kind - 8) == types_ref[2 * i + 1 : 2 * i + 2, :]
        onehot = jnp.concatenate([left.astype(F32), right.astype(F32)], axis=1).astype(BF16)
        s_ref[i * 16 : (i + 1) * 16, :] = jnp.dot(onehot, act, preferred_element_type=F32)

    normalise(0)
    wload.wait()
    for i in range(NCHUNK):
        first_dot(i)
        if i + 1 < NCHUNK:
            normalise(i + 1)
        if i >= 1:
            activate(i - 1)
    activate(NCHUNK - 1)

    lanes16 = lax.broadcasted_iota(jnp.int32, (16, LANES), 1)
    subs16 = lax.broadcasted_iota(jnp.int32, (16, LANES), 0)
    diagonal = lanes16 == subs16
    net = jnp.sum(s_ref[...].reshape(ROWS, 8, D) * q_ref[...][None], axis=1)
    net = jnp.sum(net, axis=1, keepdims=True)
    net = jnp.concatenate([net, jnp.zeros((16 - ROWS, 1), F32)], axis=0)
    net = jnp.sum(jnp.where(diagonal, net, 0.0), axis=0, keepdims=True)
    mine_ref[...] = jnp.zeros_like(mine_ref)
    mine_ref[0:1, 0:ROWS] = band_ref[...].astype(F32)
    mine_ref[1:2, 0:ROWS] = target_ref[...]
    lane1 = lax.broadcasted_iota(jnp.int32, (1, LANES), 1)
    coslat = jnp.cos(math.pi * (mine_ref[0:1, :] / 720.0 - 0.5))
    coslat = jnp.where(lane1 < ROWS, coslat, 0.0)
    mine_ref[0:1, :] = coslat * net * (1.0 / (NLON * COLS))

    pl.semaphore_wait(barrier, (NLON - 1) + (NZ - 1) + (NY - 1))
    sent = []

    def launch(copy):
        copy.start()
        sent.append(copy)
        return copy

    ex1 = [
        launch(remote(mine_ref, ex1_ref.at[lon], ex1_s.at[k - 1], ex1_r.at[k - 1], lon=lax.rem(lon + k, NLON)))
        for k in range(1, NLON)
    ]
    ex1_ref[lon] = mine_ref[...]

    def unscaled(i):
        rows = chunk_rows(i)
        kinds = tcol_ref[rows, :]
        is_one = kinds == 1.0
        is_two = kinds == 2.0
        inner = jnp.zeros((CHUNK, LANES), F32)
        for tile in range(TILES):
            cols = slice(tile * LANES, (tile + 1) * LANES)
            before = v_ref[rows, cols]
            p = before + bias_ref[0:1, cols]
            sigma = 0.5 * jnp.tanh(0.5 * p) + 0.5
            slope = sigma + (p * sigma) * (1.0 - sigma)
            weight = jnp.where(is_one, q_ref[1:2, cols], jnp.where(is_two, q_ref[2:3, cols], q_ref[0:1, cols]))
            grad = slope * weight
            inner += grad * before
            b_ref[2 * i : 2 * i + 2, cols] = jnp.sum(grad.reshape(2, COLS, LANES), axis=1)
            u_ref[rows, cols] = grad.astype(BF16)
        inv = inv_ref[rows, :]
        inner = jnp.sum(inner, axis=1, keepdims=True)
        coef_ref[rows, :] = inv * inv * (inner * (1.0 / D))

    def turn(i):
        rows = chunk_rows(i)
        nt_ref[:, rows] = n_ref[rows, :].T

    for i in range(NCHUNK // 2):
        unscaled(i)
        turn(i)
    for copy in ex1:
        copy.wait_recv()
    line = ex1_ref[0]
    for k in range(1, NLON):
        line = line + ex1_ref[k]
    sub8 = lax.broadcasted_iota(jnp.int32, (8, LANES), 0)
    line_ref[...] = jnp.where(sub8 == 0, line, mine_ref[...])
    ex2 = [
        launch(remote(line_ref, ex2_ref.at[z], ex2_s.at[k - 1], ex2_r.at[k - 1], lat=lax.rem(z + k, NZ)))
        for k in range(1, NZ)
    ]
    ex2_ref[z] = line_ref[...]
    for i in range(NCHUNK // 2, NCHUNK):
        unscaled(i)
        turn(i)
    for copy in ex2:
        copy.wait_recv()

    lanes8 = lax.broadcasted_iota(jnp.int32, (8, LANES), 1)
    weighted = jnp.concatenate([ex2_ref[k][0:1, :] for k in range(NZ)], axis=0)
    targets = jnp.concatenate([ex2_ref[k][1:2, :] for k in range(NZ)], axis=0)
    above_lane = lax.broadcasted_iota(jnp.int32, (LANES, LANES), 0)
    here_lane = lax.broadcasted_iota(jnp.int32, (LANES, LANES), 1)
    upto = (above_lane <= here_lane).astype(F32)
    local = jnp.dot(weighted, upto, precision=HIGH, preferred_element_type=F32)
    totals = jnp.sum(weighted, axis=1, keepdims=True)
    before8 = (lax.broadcasted_iota(jnp.int32, (8, 8), 1) < lax.broadcasted_iota(jnp.int32, (8, 8), 0)).astype(F32)
    below = jnp.dot(before8, jnp.broadcast_to(totals, (8, LANES)), precision=HIGH, preferred_element_type=F32)
    misfit = jnp.where(lanes8 < ROWS, local + below - targets, 0.0)
    onward = (above_lane >= here_lane).astype(F32)
    from_here = jnp.dot(misfit, onward, precision=HIGH, preferred_element_type=F32)
    north = jnp.where(sub8 > z, jnp.sum(misfit, axis=1, keepdims=True), jnp.where(sub8 == z, from_here, 0.0))
    southward = jnp.sum(north, axis=0, keepdims=True)
    flux = coslat * southward * (1.0 / (ROWS * NZ))
    flux = jnp.sum(jnp.where(diagonal, flux, 0.0), axis=1, keepdims=True)
    fb_ref[...] = jnp.broadcast_to(flux, (16, LANES))

    for r in range(ROWS):
        rows = pl.ds(r * COLS, COLS)
        scale = fb_ref[r : r + 1, 0:1]
        u_ref[rows, :] = (u_ref[rows, :].astype(F32) * scale).astype(BF16)

    def hidden_tile(half, j):
        cols = pl.ds(pl.multiple_of(half * 512 + j * 256, 256), 256)
        tile = jnp.dot(nt_ref[...], u_ref[:, cols], preferred_element_type=F32)
        return tile.reshape(NY, NX, 64, 256)

    to_core = []
    for j in range(2):
        give_ref[j] = hidden_tile(1 - core, j)
        to_core.append(
            launch(remote(give_ref.at[j], take_ref.at[j], core_s.at[j], core_r.at[j], lon=x * 2 + 1 - core))
        )
    for j in range(2):
        own_ref[j] = hidden_tile(core, j)

    def place(j):
        return y if j == 0 else x

    def toward(j, step):
        if j == 0:
            return {"mem": lax.rem(y + step, NY)}
        return {"lon": lon_at(step)}

    def block(j, owner, half):
        rows = pl.ds(32 * half, 32)
        if j == 0:
            return own_ref.at[j, owner, :, rows, :]
        return own_ref.at[j, :, owner, rows, :]

    passes, plains, aggs = {}, {}, {}
    for j in range(2):
        to_core[j].wait_recv()
        own_ref[j] = own_ref[j] + take_ref[j]
        me = place(j)
        opposite = lax.rem(me + 2, 4)
        following, previous = lax.rem(me + 1, 4), lax.rem(me + 3, 4)
        passes[j, 0] = launch(
            remote(block(j, opposite, 0), pass_ref.at[j, 0], r4_s.at[j, 0], r4_r.at[j, 0], **toward(j, 1))
        )
        passes[j, 1] = launch(
            remote(block(j, opposite, 1), pass_ref.at[j, 1], r4_s.at[j, 1], r4_r.at[j, 1], **toward(j, 3))
        )
        plains[j, 1] = launch(
            remote(block(j, following, 1), plain_ref.at[j, 1], r4_s.at[j, 2], r4_r.at[j, 2], **toward(j, 1))
        )
        plains[j, 0] = launch(
            remote(block(j, previous, 0), plain_ref.at[j, 0], r4_s.at[j, 3], r4_r.at[j, 3], **toward(j, 3))
        )

    gacc_ref[...] = jnp.zeros_like(gacc_ref)
    stores = []

    def latent_grad(i):
        rows = chunk_rows(i)
        back = lax.dot_general(u_ref[rows, :], w1_ref[...], dims, preferred_element_type=F32)
        inv = inv_ref[rows, :]
        coef = coef_ref[rows, :]
        coef = jnp.concatenate(
            [coef[k * COLS : (k + 1) * COLS] * fb_ref[2 * i + k : 2 * i + k + 1, :] for k in range(2)], axis=0
        )
        for tile in range(TILES):
            cols = slice(tile * LANES, (tile + 1) * LANES)
            xf = x_ref[rows, cols].astype(F32)
            scaled = back[:, cols] * inv
            gacc_ref[:, cols] += jnp.sum((scaled * xf).reshape(CHUNK // 8, 8, LANES), axis=0)
            stage_ref[rows, cols] = (scaled * gain_ref[0:1, cols] - xf * coef).astype(BF16)
        store = pltpu.make_async_copy(stage_ref.at[rows], outlat_hbm.at[rows], osem.at[i])
        store.start()
        stores.append(store)

    for i in range(NCHUNK // 2):
        latent_grad(i)

    for j in range(2):
        me = place(j)
        for half, step in ((0, 1), (1, 3)):
            passes[j, half].wait_recv()
            mid = block(j, lax.rem(me + step, 4), half)
            mid[...] = mid[...] + pass_ref[j, half]
            aggs[j, half] = launch(
                remote(mid, agg_ref.at[j, half], r4_s.at[j, 4 + half], r4_r.at[j, 4 + half], **toward(j, step))
            )

    for i in range(NCHUNK // 2, NCHUNK):
        latent_grad(i)

    small = jnp.zeros((8, D), F32)
    bias_sum = jnp.zeros((1, D), F32)
    for r in range(ROWS):
        scale = fb_ref[r : r + 1, 0:1]
        small = small + s_ref[r * 8 : (r + 1) * 8, :] * scale
        bias_sum = bias_sum + b_ref[r : r + 1, :] * scale
    gain_sum = jnp.sum(gacc_ref[...], axis=0, keepdims=True)
    row8 = lax.broadcasted_iota(jnp.int32, (8, D), 0)
    small = jnp.where(row8 == 3, bias_sum, jnp.where(row8 == 4, gain_sum, small))
    for k in range(NLON):
        sm_ref[k] = small[:, k * LANES : (k + 1) * LANES]
    sm1 = []
    for k in range(1, NLON):
        peer = lax.rem(lon + k, NLON)
        sm1.append(launch(remote(sm_ref.at[peer], sm1_ref.at[lon], sm1_s.at[k - 1], sm1_r.at[k - 1], lon=peer)))
    sm1_ref[lon] = sm_ref[lon]

    crosses = []
    for j in range(2):
        for half in range(2):
            plains[j, half].wait_recv()
            aggs[j, half].wait_recv()
            kept = block(j, place(j), half)
            part_ref[j, :, 32 * half : 32 * (half + 1), :] = kept[...] + plain_ref[j, half] + agg_ref[j, half]
        other = 1 - j
        for k in range(1, 4):
            peer = lax.rem(place(other) + k, 4)
            crosses.append(
                launch(
                    remote(
                        part_ref.at[j, peer],
                        cross_ref.at[j, k - 1],
                        cross_s.at[j, k - 1],
                        cross_r.at[j, k - 1],
                        **toward(other, k),
                    )
                )
            )

    for copy in sm1:
        copy.wait_recv()
    total = sm1_ref[0]
    for k in range(1, NLON):
        total = total + sm1_ref[k]
    t1_ref[...] = total
    sm2 = [
        launch(remote(t1_ref, sm2_ref.at[z], sm2_s.at[k - 1], sm2_r.at[k - 1], lat=lax.rem(z + k, NZ)))
        for k in range(1, NZ)
    ]
    sm2_ref[z] = t1_ref[...]

    depths = []
    for j in range(2):
        for k in range(3):
            crosses[3 * j + k].wait_recv()
        piece = part_ref[j, place(1 - j)] + cross_ref[j, 0] + cross_ref[j, 1] + cross_ref[j, 2]
        piece_ref[j] = piece.reshape(NZ, 8, 256)
        for k in range(1, NZ):
            peer = lax.rem(z + k, NZ)
            depths.append(
                launch(
                    remote(
                        piece_ref.at[j, peer],
                        depth_ref.at[j, k - 1],
                        depth_s.at[j, k - 1],
                        depth_r.at[j, k - 1],
                        lat=peer,
                    )
                )
            )

    for copy in sm2:
        copy.wait_recv()
    total = sm2_ref[0]
    for k in range(1, NZ):
        total = total + sm2_ref[k]
    t2_ref[...] = total
    sm3 = [
        launch(remote(t2_ref, sm3_ref.at[y], sm3_s.at[k - 1], sm3_r.at[k - 1], mem=lax.rem(y + k, NY)))
        for k in range(1, NY)
    ]
    sm3_ref[y] = t2_ref[...]

    agz = []
    for j in range(2):
        for k in range(NZ - 1):
            depths[(NZ - 1) * j + k].wait_recv()
        piece = piece_ref[j, z]
        for k in range(NZ - 1):
            piece = piece + depth_ref[j, k]
        rows = pl.ds(pl.multiple_of(x * 64 + z * 8, 8), 8)
        hid_ref[core, j, rows, :] = piece
        spot = hid_ref.at[core, j, rows, :]
        for k in range(1, NZ):
            agz.append(
                launch(remote(spot, spot, agz_s.at[j, k - 1], agz_r.at[j, k - 1], lat=lax.rem(z + k, NZ)))
            )

    for copy in sm3:
        copy.wait_recv()
    total = sm3_ref[0]
    for k in range(1, NY):
        total = total + sm3_ref[k]
    smo_ref[lon] = total
    sm4 = [
        launch(remote(smo_ref.at[lon], smo_ref.at[lon], sm4_s.at[k - 1], sm4_r.at[k - 1], lon=lax.rem(lon + k, NLON)))
        for k in range(1, NLON)
    ]

    def span(step, half):
        start = lax.rem(x + step, NX) * 64
        if half is None:
            return hid_ref.at[core, :, pl.ds(pl.multiple_of(start, 64), 64), :]
        return hid_ref.at[core, :, pl.ds(pl.multiple_of(start + 32 * half, 32), 32), :]

    sibling = x * 2 + 1 - core
    for copy in agz:
        copy.wait_recv()
    right = launch(remote(span(0, None), span(0, None), agx_s.at[0], agx_r.at[0], lon=lon_at(1)))
    left = launch(remote(span(0, None), span(0, None), agx_s.at[1], agx_r.at[1], lon=lon_at(3)))
    agc = [launch(remote(span(0, None), span(0, None), agc_s.at[0], agc_r.at[0], lon=sibling))]
    right.wait_recv()
    on_right = launch(remote(span(3, 0), span(3, 0), agx_s.at[2], agx_r.at[2], lon=lon_at(1)))
    agc.append(launch(remote(span(3, None), span(3, None), agc_s.at[1], agc_r.at[1], lon=sibling)))
    left.wait_recv()
    on_left = launch(remote(span(1, 1), span(1, 1), agx_s.at[3], agx_r.at[3], lon=lon_at(3)))
    agc.append(launch(remote(span(1, None), span(1, None), agc_s.at[2], agc_r.at[2], lon=sibling)))

    for copy in sm4:
        copy.wait_recv()
    for k in range(NLON):
        cols = slice(k * LANES, (k + 1) * LANES)
        outbias_ref[0:1, cols] = smo_ref[k][3:4, :]
        outgain_ref[0:1, cols] = smo_ref[k][4:5, :]
        outw_ref[cols, :] = lax.dot_general(
            smo_ref[k], tab_ref[...], (((0,), (0,)), ((), ())), precision=HIGH, preferred_element_type=F32
        )

    on_right.wait_recv()
    agc.append(launch(remote(span(2, 0), span(2, 0), agc_s.at[3], agc_r.at[3], lon=sibling)))
    on_left.wait_recv()
    agc.append(launch(remote(span(2, 1), span(2, 1), agc_s.at[4], agc_r.at[4], lon=sibling)))
    for copy in agc:
        copy.wait_recv()
    out = []
    for half in range(2):
        for j in range(2):
            cols = pl.ds(half * 512 + j * 256, 256)
            copy = pltpu.make_async_copy(hid_ref.at[half, j], outhid_hbm.at[:, cols], hsem.at[half, j])
            copy.start()
            out.append(copy)
    for copy in sent:
        copy.wait_send()
    for copy in stores:
        copy.wait()
    for copy in out:
        copy.wait()


def on_device(latent, norm_gain, hidden_weight, hidden_bias, output_weight, flux_table, target, land_sea, band_index):
    vmem = pl.BlockSpec(memory_space=pltpu.VMEM)
    hbm = pl.BlockSpec(memory_space=pl.ANY)
    dma = pltpu.SemaphoreType.DMA
    scratch = [
        pltpu.VMEM((CELLS, D), BF16),
        pltpu.VMEM((D, D), BF16),
        pltpu.VMEM((CELLS, D), BF16),
        pltpu.VMEM((D, CELLS), BF16),
        pltpu.VMEM((CELLS, D), F32),
        pltpu.VMEM((CELLS, D), BF16),
        pltpu.VMEM((CELLS, LANES), F32),
        pltpu.VMEM((CELLS, LANES), F32),
        pltpu.VMEM((CELLS, LANES), F32),
        pltpu.VMEM((LANES, LANES), F32),
        pltpu.VMEM((8, D), F32),
        pltpu.VMEM((8, 80), F32),
        pltpu.VMEM((ROWS * 8, D), F32),
        pltpu.VMEM((16, D), F32),
        pltpu.VMEM((16, LANES), F32),
        pltpu.VMEM((8, D), F32),
        pltpu.VMEM((CELLS, D), BF16),
        pltpu.VMEM((8, LANES), F32),
        pltpu.VMEM((NLON, 8, LANES), F32),
        pltpu.VMEM((8, LANES), F32),
        pltpu.VMEM((NZ, 8, LANES), F32),
        pltpu.VMEM((2, NY, NX, 64, 256), F32),
        pltpu.VMEM((2, NY, NX, 64, 256), F32),
        pltpu.VMEM((2, NY, NX, 64, 256), F32),
        pltpu.VMEM((2, 2, 4, 32, 256), F32),
        pltpu.VMEM((2, 2, 4, 32, 256), F32),
        pltpu.VMEM((2, 2, 4, 32, 256), F32),
        pltpu.VMEM((2, 4, 64, 256), F32),
        pltpu.VMEM((2, 3, 64, 256), F32),
        pltpu.VMEM((2, NZ, 8, 256), F32),
        pltpu.VMEM((2, NZ - 1, 8, 256), F32),
        pltpu.VMEM((2, 2, 256, 256), F32),
        pltpu.VMEM((NLON, 8, LANES), F32),
        pltpu.VMEM((NLON, 8, LANES), F32),
        pltpu.VMEM((8, LANES), F32),
        pltpu.VMEM((NZ, 8, LANES), F32),
        pltpu.VMEM((8, LANES), F32),
        pltpu.VMEM((NY, 8, LANES), F32),
        pltpu.VMEM((NLON, 8, LANES), F32),
        dma((NCHUNK,)),
        dma,
        dma((NCHUNK,)),
        dma((2, 2)),
        dma((7,)), dma((7,)),
        dma((7,)), dma((7,)),
        dma((2,)), dma((2,)),
        dma((2, 6)), dma((2, 6)),
        dma((2, 3)), dma((2, 3)),
        dma((2, 7)), dma((2, 7)),
        dma((2, 7)), dma((2, 7)),
        dma((4,)), dma((4,)),
        dma((5,)), dma((5,)),
        dma((7,)), dma((7,)),
        dma((7,)), dma((7,)),
        dma((3,)), dma((3,)),
        dma((7,)), dma((7,)),
    ]
    grad_cells, grad_hidden, grad_out, grad_gain, grad_bias = pl.pallas_call(
        kernel,
        out_shape=(
            jax.ShapeDtypeStruct((CELLS, D), BF16),
            jax.ShapeDtypeStruct((D // NY, D), F32),
            jax.ShapeDtypeStruct((D, 80), F32),
            jax.ShapeDtypeStruct((1, D), F32),
            jax.ShapeDtypeStruct((1, D), F32),
        ),
        in_specs=[hbm, vmem, hbm, vmem, vmem, vmem, vmem, vmem, vmem],
        out_specs=(hbm, hbm, vmem, vmem, vmem),
        scratch_shapes=scratch,
        compiler_params=pltpu.CompilerParams(
            collective_id=0, has_side_effects=True, vmem_limit_bytes=60 * 1024 * 1024
        ),
        cost_estimate=pl.CostEstimate(flops=10_000_000_000, bytes_accessed=9_000_000, transcendentals=3_000_000),
    )(
        latent.reshape(CELLS, D),
        norm_gain.reshape(1, D),
        hidden_weight,
        hidden_bias.reshape(1, D),
        output_weight,
        flux_table,
        target,
        land_sea,
        band_index.reshape(1, ROWS),
    )
    return (
        grad_cells.reshape(latent.shape),
        grad_hidden,
        grad_out,
        grad_gain.reshape(D),
        grad_bias.reshape(D),
    )


def solution(mesh):
    return jax.shard_map(
        on_device,
        mesh=mesh,
        in_specs=(
            P("mem", "lat", "lon", None),
            P(),
            P(),
            P(),
            P(),
            P(),
            P("mem", "lat"),
            P("lat", "lon"),
            P("lat"),
        ),
        out_specs=(P("mem", "lat", "lon", None), P("mem", None), P(), P(), P()),
        check_vma=False,
    )
```

time: 392 us -> 82.9 us (0.21)
  waiting for transfers between devices: 177 us -> 0 us
  blocking collectives: 125 us -> 0 us
  Pallas kernels: 0 us -> 72.2 us
  matrix products: 31.3 us -> 0 us
  between operations: 14.2 us -> 0.65 us
  other arithmetic: 11.7 us -> 0 us
  local copies, waits for them, and re-layouts: 20.9 us -> 9.83 us
  loops' own time: 10.6 us -> 0 us
    psum x1 -> x0, waiting for transfers between devices: 177 us -> none  [on_device(): lax.psum((grad_hidden, grad_out, grad_gain, grad_bias), ('lat', 'lon', 'm...]
    psum x2 -> x0, blocking collectives: 100 us -> none  [the longest x1 85 us: on_device(): lax.psum((grad_hidden, grad_out, grad_gain, grad_bias), ('lat', 'lon', 'm...]
    pallas_call x0 -> x1, Pallas kernels: none -> 72.2 us  [on_device(): pl.pallas_call(kernel, out_shape=(jax.ShapeDtypeStruct((CELLS, D), BF16),...]
    dot_general x7 -> x0, matrix products: 31.3 us -> none  [the longest x1 8.9 us: on_device(): lax.dot_general(preact_grad, hidden_weight, (((1,), (1,)), ((), ())), pre...]
    unnamed x2 -> x0, blocking collectives: 25.2 us -> none
    dynamic_slice x17 -> x0, local copies, waits for them, and re-layouts: 12.6 us -> none  [the longest x16 10.3 us: step(): new = combine(before, everything[at])]
    another operation x2 -> x0, loops' own time: 10.6 us -> none  [prefix(): return lax.fori_loop(0, count, step, start)]
    convert_element_type x2 -> x0, other arithmetic: 8.39 us -> none  [the longest x1 5.72 us: on_device(): grad_cells.astype(jnp.bfloat16)]
  transfers between devices with their start and end apart: 1 -> 0, of which waited for: 1 -> 0; matrix products, arithmetic and copies ran while one was open for 4% -> 0% of each run, Pallas kernels for 0% -> 0%
where the time goes in v1:
time: 82.9 us; the launch traced here: 82.7 us
  Pallas kernels  72.2 us (87%)
  local copies, waits for them, and re-layouts  9.83 us (12%)
    pallas_call x1, Pallas kernels, on_device(): pl.pallas_call(kernel, out_shape=(jax.ShapeDtypeStruct((CELLS, D), BF16),...  72.2 us
    unnamed x12, local copies, waits for them, and re-layouts  9.83 us

profile of v1, /device:TPU:1, one launch (start us, length us, event | category | flops | bytes accessed | tf_op | source)
XLA Modules:
  0.0 82.7 jit_solution(9944796534131064617)
XLA Ops:
  0.6 1.8 %copy.14.w2_ref = bf16[1024,80]{1,0:T(8,128)(2,1)} copy(bf16[1024,80]{0,1:T(8,128)(2,1)} %param.13) | data formatting | bytes 327680 | tf_op args[4]
  2.4 72.2 %shard_map.128 = (bf16[1536,1024]{1,0:T(8,128)(2,1)}, f32[256,1024]{1,0:T(8,128)}, f32[1024,80]{1,0:T(8,128)}, f32[1,1024]{1,0:T(1,128)}, f32[1,1024]{1,0:T(1,128)}) custom-call(bf16[1536,1024]{1,0:T(8,128)(2,1)} %bitcast.10, f32[1,1024]{1,0:T(1,128)} %bitcast.11, bf16[1024,1024]{1,0:T(8,128)(2,1)} %w1_hbm.1, f32[1,1024]{1,0:T(1,128)} %bitcast.12, ...), custom_call_target="tpu_custom_call" | custom-call | flops 10000000000 | bytes 9000000 | tf_op jit(solution)/shard_map/pallas_call | solution.py:535
  74.6 2.0 %copy.15 = f32[1024,80]{0,1:T(8,128)} copy(f32[1024,80]{1,0:T(8,128)} %get-tuple-element.17) | data formatting | bytes 655360
  76.6 0.0 copy-start
  76.6 0.0 copy-start.2
  76.6 0.0 copy-start.1
  76.6 3.9 %copy.20 = bf16[1,12,128,1024]{3,2,1,0:T(8,128)(2,1)} copy(bf16[1,12,128,1024]{3,2,1,0:T(8,128)(2,1)} %bitcast.7) | data formatting | bytes 6291456
  80.5 0.0 copy-done
  80.5 1.0 %copy.21 = f32[256,1024]{1,0:T(8,128)} copy(f32[256,1024]{1,0:T(8,128)S(1)} %copy-done) | data formatting | bytes 2097152
  81.5 0.0 copy-done.2
  81.5 0.6 copy.22
  82.1 0.0 copy-done.1
  82.1 0.6 copy.23
Async XLA Ops:
  76.6 4.0 %copy-start = (f32[256,1024]{1,0:T(8,128)S(1)}, f32[256,1024]{1,0:T(8,128)}, u32[]{:S(2)}) copy-start(f32[256,1024]{1,0:T(8,128)} %get-tuple-element.26) | copy-start | bytes 3145732
  76.6 4.9 %copy-start.2 = (f32[1,1024]{1,0:T(1,128)S(1)}, f32[1,1024]{1,0:T(1,128)}, u32[]{:S(2)}) copy-start(f32[1,1024]{1,0:T(1,128)} %get-tuple-element.13) | copy-start | bytes 12292
  76.6 5.5 %copy-start.1 = (f32[1,1024]{1,0:T(1,128)S(1)}, f32[1,1024]{1,0:T(1,128)}, u32[]{:S(2)}) copy-start(f32[1,1024]{1,0:T(1,128)} %get-tuple-element.14) | copy-start | bytes 12292

commit v2 on v1

--- a/solution.py
+++ b/solution.py
@@ -37,14 +37,14 @@
 
 def kernel(
     lat_hbm, gain_ref, w1_hbm, bias_ref, w2_ref, table_ref, target_ref, types_ref, band_ref,
-    outlat_hbm, outhid_hbm, outw_ref, outgain_ref, outbias_ref,
+    outlat_ref, outhid_ref, outw_ref, outgain_ref, outbias_ref,
     x_ref, w1_ref, n_ref, nt_ref, v_ref, u_ref, inv_ref, coef_ref, tcol_ref, square_ref,
-    q_ref, tab_ref, s_ref, b_ref, fb_ref, gacc_ref, stage_ref,
+    q_ref, tab_ref, s_ref, b_ref, fb_ref, gacc_ref,
     mine_ref, ex1_ref, line_ref, ex2_ref,
-    give_ref, take_ref, own_ref, pass_ref, plain_ref, agg_ref, part_ref, cross_ref, piece_ref, depth_ref,
+    give_ref, take_ref, own_ref, first_ref, part_ref, cross_ref, piece_ref, depth_ref,
     hid_ref, sm_ref, sm1_ref, t1_ref, sm2_ref, t2_ref, sm3_ref, smo_ref,
-    xsem, wsem, osem, hsem,
-    ex1_s, ex1_r, ex2_s, ex2_r, core_s, core_r, r4_s, r4_r, cross_s, cross_r, depth_s, depth_r,
+    xsem, wsem,
+    ex1_s, ex1_r, ex2_s, ex2_r, core_s, core_r, first_s, first_r, cross_s, cross_r, depth_s, depth_r,
     agz_s, agz_r, agx_s, agx_r, agc_s, agc_r, sm1_s, sm1_r, sm2_s, sm2_r, sm3_s, sm3_r, sm4_s, sm4_r,
 ):
     z = lax.axis_index("lat")
@@ -81,7 +81,7 @@
     rest = table - high.astype(F32)
     middle = rest.astype(BF16)
     w2 = w2_ref[...]
-    dims = (((1,), (1,)), ((), ()))
+    dims = (((1,), (0,)), ((), ()))
     q_ref[...] = lax.dot_general(high, w2, dims, preferred_element_type=F32) + lax.dot_general(
         middle, w2, dims, preferred_element_type=F32
     )
@@ -226,60 +226,55 @@
         scale = fb_ref[r : r + 1, 0:1]
         u_ref[rows, :] = (u_ref[rows, :].astype(F32) * scale).astype(BF16)
 
-    def hidden_tile(half, j):
-        cols = pl.ds(pl.multiple_of(half * 512 + j * 256, 256), 256)
+    def hidden_tile(ref, half, t):
+        cols = pl.ds(pl.multiple_of(half * 512 + t * 256, 256), 256)
         tile = jnp.dot(nt_ref[...], u_ref[:, cols], preferred_element_type=F32)
-        return tile.reshape(NY, NX, 64, 256)
+        for way in range(2):
+            ref[t, way] = tile[:, way * LANES : (way + 1) * LANES].reshape(NY, NX, 64, LANES)
+
+    sibling = x * 2 + 1 - core
 
     to_core = []
-    for j in range(2):
-        give_ref[j] = hidden_tile(1 - core, j)
-        to_core.append(
-            launch(remote(give_ref.at[j], take_ref.at[j], core_s.at[j], core_r.at[j], lon=x * 2 + 1 - core))
-        )
-    for j in range(2):
-        own_ref[j] = hidden_tile(core, j)
-
-    def place(j):
-        return y if j == 0 else x
-
-    def toward(j, step):
-        if j == 0:
+    for t in range(2):
+        hidden_tile(give_ref, 1 - core, t)
+        to_core.append(launch(remote(give_ref.at[t], take_ref.at[t], core_s.at[t], core_r.at[t], lon=sibling)))
+    for t in range(2):
+        hidden_tile(own_ref, core, t)
+
+    def place(way):
+        return y if way == 0 else x
+
+    def toward(way, step):
+        if way == 0:
             return {"mem": lax.rem(y + step, NY)}
         return {"lon": lon_at(step)}
 
-    def block(j, owner, half):
-        rows = pl.ds(32 * half, 32)
-        if j == 0:
-            return own_ref.at[j, owner, :, rows, :]
-        return own_ref.at[j, :, owner, rows, :]
-
-    passes, plains, aggs = {}, {}, {}
-    for j in range(2):
-        to_core[j].wait_recv()
-        own_ref[j] = own_ref[j] + take_ref[j]
-        me = place(j)
-        opposite = lax.rem(me + 2, 4)
-        following, previous = lax.rem(me + 1, 4), lax.rem(me + 3, 4)
-        passes[j, 0] = launch(
-            remote(block(j, opposite, 0), pass_ref.at[j, 0], r4_s.at[j, 0], r4_r.at[j, 0], **toward(j, 1))
-        )
-        passes[j, 1] = launch(
-            remote(block(j, opposite, 1), pass_ref.at[j, 1], r4_s.at[j, 1], r4_r.at[j, 1], **toward(j, 3))
-        )
-        plains[j, 1] = launch(
-            remote(block(j, following, 1), plain_ref.at[j, 1], r4_s.at[j, 2], r4_r.at[j, 2], **toward(j, 1))
-        )
-        plains[j, 0] = launch(
-            remote(block(j, previous, 0), plain_ref.at[j, 0], r4_s.at[j, 3], r4_r.at[j, 3], **toward(j, 3))
-        )
+    def share(t, way, owner):
+        return own_ref.at[t, way, owner] if way == 0 else own_ref.at[t, way, :, owner]
+
+    firsts = {}
+    for t in range(2):
+        to_core[t].wait_recv()
+        own_ref[t] = own_ref[t] + take_ref[t]
+        for way in range(2):
+            for k in (2, 1, 3):
+                firsts[t, way, k] = launch(
+                    remote(
+                        share(t, way, lax.rem(place(way) + k, 4)),
+                        first_ref.at[t, way, k - 1],
+                        first_s.at[t, way, k - 1],
+                        first_r.at[t, way, k - 1],
+                        **toward(way, k),
+                    )
+                )
 
     gacc_ref[...] = jnp.zeros_like(gacc_ref)
-    stores = []
 
     def latent_grad(i):
         rows = chunk_rows(i)
-        back = lax.dot_general(u_ref[rows, :], w1_ref[...], dims, preferred_element_type=F32)
+        back = lax.dot_general(
+            u_ref[rows, :], w1_ref[...], (((1,), (1,)), ((), ())), preferred_element_type=F32
+        )
         inv = inv_ref[rows, :]
         coef = coef_ref[rows, :]
         coef = jnp.concatenate(
@@ -290,25 +285,9 @@
             xf = x_ref[rows, cols].astype(F32)
             scaled = back[:, cols] * inv
             gacc_ref[:, cols] += jnp.sum((scaled * xf).reshape(CHUNK // 8, 8, LANES), axis=0)
-            stage_ref[rows, cols] = (scaled * gain_ref[0:1, cols] - xf * coef).astype(BF16)
-        store = pltpu.make_async_copy(stage_ref.at[rows], outlat_hbm.at[rows], osem.at[i])
-        store.start()
-        stores.append(store)
-
-    for i in range(NCHUNK // 2):
-        latent_grad(i)
-
-    for j in range(2):
-        me = place(j)
-        for half, step in ((0, 1), (1, 3)):
-            passes[j, half].wait_recv()
-            mid = block(j, lax.rem(me + step, 4), half)
-            mid[...] = mid[...] + pass_ref[j, half]
-            aggs[j, half] = launch(
-                remote(mid, agg_ref.at[j, half], r4_s.at[j, 4 + half], r4_r.at[j, 4 + half], **toward(j, step))
-            )
-
-    for i in range(NCHUNK // 2, NCHUNK):
+            outlat_ref[rows, cols] = (scaled * gain_ref[0:1, cols] - xf * coef).astype(BF16)
+
+    for i in range(NCHUNK):
         latent_grad(i)
 
     small = jnp.zeros((8, D), F32)
@@ -328,28 +307,97 @@
         sm1.append(launch(remote(sm_ref.at[peer], sm1_ref.at[lon], sm1_s.at[k - 1], sm1_r.at[k - 1], lon=peer)))
     sm1_ref[lon] = sm_ref[lon]
 
-    crosses = []
-    for j in range(2):
-        for half in range(2):
-            plains[j, half].wait_recv()
-            aggs[j, half].wait_recv()
-            kept = block(j, place(j), half)
-            part_ref[j, :, 32 * half : 32 * (half + 1), :] = kept[...] + plain_ref[j, half] + agg_ref[j, half]
-        other = 1 - j
-        for k in range(1, 4):
-            peer = lax.rem(place(other) + k, 4)
-            crosses.append(
-                launch(
+    crosses, depths, agz = {}, {}, {}
+
+    def cross(t):
+        for way in range(2):
+            for k in range(1, 4):
+                firsts[t, way, k].wait_recv()
+            part_ref[t, way] = (
+                share(t, way, place(way))[...] + first_ref[t, way, 0] + first_ref[t, way, 1] + first_ref[t, way, 2]
+            )
+            other = 1 - way
+            for k in (2, 1, 3):
+                crosses[t, way, k] = launch(
                     remote(
-                        part_ref.at[j, peer],
-                        cross_ref.at[j, k - 1],
-                        cross_s.at[j, k - 1],
-                        cross_r.at[j, k - 1],
+                        part_ref.at[t, way, lax.rem(place(other) + k, 4)],
+                        cross_ref.at[t, way, k - 1],
+                        cross_s.at[t, way, k - 1],
+                        cross_r.at[t, way, k - 1],
                         **toward(other, k),
                     )
                 )
+
+    by_distance = (4, 3, 5, 2, 6, 1, 7)
+
+    def deepen(t):
+        for way in range(2):
+            for k in range(1, 4):
+                crosses[t, way, k].wait_recv()
+            piece = part_ref[t, way, place(1 - way)] + cross_ref[t, way, 0] + cross_ref[t, way, 1] + cross_ref[t, way, 2]
+            piece_ref[t, :, way] = piece.reshape(NZ, 8, LANES)
+        for k in by_distance:
+            peer = lax.rem(z + k, NZ)
+            depths[t, k] = launch(
+                remote(
+                    piece_ref.at[t, peer], depth_ref.at[t, k - 1], depth_s.at[t, k - 1], depth_r.at[t, k - 1], lat=peer
+                )
             )
 
+    slots = (0, 1, 7, 2, 6, 3, 5, 4)
+    slot_of = {k: slots.index(k) for k in range(NZ)}
+
+    def finish(t):
+        for k in range(1, NZ):
+            depths[t, k].wait_recv()
+        piece = piece_ref[t, z]
+        for k in range(NZ - 1):
+            piece = piece + depth_ref[t, k]
+        hid_ref[core, t, x, 0] = piece
+        for k in by_distance:
+            agz[t, k] = launch(
+                remote(
+                    hid_ref.at[core, t, x, 0],
+                    hid_ref.at[core, t, x, slot_of[NZ - k]],
+                    agz_s.at[t, k - 1],
+                    agz_r.at[t, k - 1],
+                    lat=lax.rem(z + k, NZ),
+                )
+            )
+
+    groups = (slice(0, 5), slice(5, 8))
+    agx, agc = {}, {}
+
+    def spread(t, g):
+        part = groups[g]
+        for k in range(1, NZ):
+            if part.start <= slot_of[NZ - k] < part.stop:
+                agz[t, k].wait_recv()
+        many = pl.ds(part.start, part.stop - part.start)
+        spot = hid_ref.at[core, t, x, many]
+        for k in (2, 1, 3):
+            agx[t, g, k] = launch(
+                remote(spot, spot, agx_s.at[t, g, k - 1], agx_r.at[t, g, k - 1], lon=lon_at(k))
+            )
+        agc[t, g, 0] = launch(remote(spot, spot, agc_s.at[t, g, 0], agc_r.at[t, g, 0], lon=sibling))
+
+    def to_sibling(t, g):
+        part = groups[g]
+        many = pl.ds(part.start, part.stop - part.start)
+        for k in (1, 3, 2):
+            agx[t, g, k].wait_recv()
+            spot = hid_ref.at[core, t, lax.rem(x + 4 - k, NX), many]
+            agc[t, g, k] = launch(remote(spot, spot, agc_s.at[t, g, k], agc_r.at[t, g, k], lon=sibling))
+
+    def place_rows(half, t):
+        for xi in range(NX):
+            for k in range(NZ):
+                rows = pl.ds(pl.multiple_of(xi * 64 + lax.rem(z + k, NZ) * 8, 8), 8)
+                for way in range(2):
+                    cols = pl.ds(pl.multiple_of(half * 512 + t * 256 + way * LANES, LANES), LANES)
+                    outhid_ref[rows, cols] = hid_ref[half, t, xi, slot_of[k], way]
+
+    cross(0)
     for copy in sm1:
         copy.wait_recv()
     total = sm1_ref[0]
@@ -358,30 +406,12 @@
     t1_ref[...] = total
     sm2 = [
         launch(remote(t1_ref, sm2_ref.at[z], sm2_s.at[k - 1], sm2_r.at[k - 1], lat=lax.rem(z + k, NZ)))
-        for k in range(1, NZ)
+        for k in by_distance
     ]
     sm2_ref[z] = t1_ref[...]
-
-    depths = []
-    for j in range(2):
-        for k in range(3):
-            crosses[3 * j + k].wait_recv()
-        piece = part_ref[j, place(1 - j)] + cross_ref[j, 0] + cross_ref[j, 1] + cross_ref[j, 2]
-        piece_ref[j] = piece.reshape(NZ, 8, 256)
-        for k in range(1, NZ):
-            peer = lax.rem(z + k, NZ)
-            depths.append(
-                launch(
-                    remote(
-                        piece_ref.at[j, peer],
-                        depth_ref.at[j, k - 1],
-                        depth_s.at[j, k - 1],
-                        depth_r.at[j, k - 1],
-                        lat=peer,
-                    )
-                )
-            )
-
+    deepen(0)
+    cross(1)
+    deepen(1)
     for copy in sm2:
         copy.wait_recv()
     total = sm2_ref[0]
@@ -393,22 +423,7 @@
         for k in range(1, NY)
     ]
     sm3_ref[y] = t2_ref[...]
-
-    agz = []
-    for j in range(2):
-        for k in range(NZ - 1):
-            depths[(NZ - 1) * j + k].wait_recv()
-        piece = piece_ref[j, z]
-        for k in range(NZ - 1):
-            piece = piece + depth_ref[j, k]
-        rows = pl.ds(pl.multiple_of(x * 64 + z * 8, 8), 8)
-        hid_ref[core, j, rows, :] = piece
-        spot = hid_ref.at[core, j, rows, :]
-        for k in range(1, NZ):
-            agz.append(
-                launch(remote(spot, spot, agz_s.at[j, k - 1], agz_r.at[j, k - 1], lat=lax.rem(z + k, NZ)))
-            )
-
+    finish(0)
     for copy in sm3:
         copy.wait_recv()
     total = sm3_ref[0]
@@ -419,54 +434,45 @@
         launch(remote(smo_ref.at[lon], smo_ref.at[lon], sm4_s.at[k - 1], sm4_r.at[k - 1], lon=lax.rem(lon + k, NLON)))
         for k in range(1, NLON)
     ]
-
-    def span(step, half):
-        start = lax.rem(x + step, NX) * 64
-        if half is None:
-            return hid_ref.at[core, :, pl.ds(pl.multiple_of(start, 64), 64), :]
-        return hid_ref.at[core, :, pl.ds(pl.multiple_of(start + 32 * half, 32), 32), :]
-
-    sibling = x * 2 + 1 - core
-    for copy in agz:
-        copy.wait_recv()
-    right = launch(remote(span(0, None), span(0, None), agx_s.at[0], agx_r.at[0], lon=lon_at(1)))
-    left = launch(remote(span(0, None), span(0, None), agx_s.at[1], agx_r.at[1], lon=lon_at(3)))
-    agc = [launch(remote(span(0, None), span(0, None), agc_s.at[0], agc_r.at[0], lon=sibling))]
-    right.wait_recv()
-    on_right = launch(remote(span(3, 0), span(3, 0), agx_s.at[2], agx_r.at[2], lon=lon_at(1)))
-    agc.append(launch(remote(span(3, None), span(3, None), agc_s.at[1], agc_r.at[1], lon=sibling)))
-    left.wait_recv()
-    on_left = launch(remote(span(1, 1), span(1, 1), agx_s.at[3], agx_r.at[3], lon=lon_at(3)))
-    agc.append(launch(remote(span(1, None), span(1, None), agc_s.at[2], agc_r.at[2], lon=sibling)))
-
+    finish(1)
+    spread(0, 0)
+    spread(0, 1)
     for copy in sm4:
         copy.wait_recv()
     for k in range(NLON):
         cols = slice(k * LANES, (k + 1) * LANES)
         outbias_ref[0:1, cols] = smo_ref[k][3:4, :]
         outgain_ref[0:1, cols] = smo_ref[k][4:5, :]
-        outw_ref[cols, :] = lax.dot_general(
-            smo_ref[k], tab_ref[...], (((0,), (0,)), ((), ())), precision=HIGH, preferred_element_type=F32
+        outw_ref[:, cols] = lax.dot_general(
+            tab_ref[...], smo_ref[k], (((0,), (0,)), ((), ())), precision=HIGH, preferred_element_type=F32
         )
-
-    on_right.wait_recv()
-    agc.append(launch(remote(span(2, 0), span(2, 0), agc_s.at[3], agc_r.at[3], lon=sibling)))
-    on_left.wait_recv()
-    agc.append(launch(remote(span(2, 1), span(2, 1), agc_s.at[4], agc_r.at[4], lon=sibling)))
-    for copy in agc:
-        copy.wait_recv()
-    out = []
-    for half in range(2):
-        for j in range(2):
-            cols = pl.ds(half * 512 + j * 256, 256)
-            copy = pltpu.make_async_copy(hid_ref.at[half, j], outhid_hbm.at[:, cols], hsem.at[half, j])
-            copy.start()
-            out.append(copy)
+    to_sibling(0, 0)
+    to_sibling(0, 1)
+    spread(1, 0)
+    spread(1, 1)
+    place_rows(core, 0)
+    to_sibling(1, 0)
+    to_sibling(1, 1)
+    for g in range(2):
+        for k in range(4):
+            agc[0, g, k].wait_recv()
+    place_rows(1 - core, 0)
+    place_rows(core, 1)
     for copy in sent:
         copy.wait_send()
-    for copy in stores:
-        copy.wait()
-    for copy in out:
+    for g in range(2):
+        for k in range(4):
+            agc[1, g, k].wait_recv()
+    place_rows(1 - core, 1)
+
+
+def write_out(*refs):
+    sems = refs[-1]
+    half = len(refs) // 2
+    copies = [pltpu.make_async_copy(refs[i], refs[half + i], sems.at[i]) for i in range(half)]
+    for copy in copies:
+        copy.start()
+    for copy in copies:
         copy.wait()
 
 
@@ -491,22 +497,19 @@
         pltpu.VMEM((16, D), F32),
         pltpu.VMEM((16, LANES), F32),
         pltpu.VMEM((8, D), F32),
-        pltpu.VMEM((CELLS, D), BF16),
         pltpu.VMEM((8, LANES), F32),
         pltpu.VMEM((NLON, 8, LANES), F32),
         pltpu.VMEM((8, LANES), F32),
         pltpu.VMEM((NZ, 8, LANES), F32),
-        pltpu.VMEM((2, NY, NX, 64, 256), F32),
-        pltpu.VMEM((2, NY, NX, 64, 256), F32),
-        pltpu.VMEM((2, NY, NX, 64, 256), F32),
-        pltpu.VMEM((2, 2, 4, 32, 256), F32),
-        pltpu.VMEM((2, 2, 4, 32, 256), F32),
-        pltpu.VMEM((2, 2, 4, 32, 256), F32),
-        pltpu.VMEM((2, 4, 64, 256), F32),
-        pltpu.VMEM((2, 3, 64, 256), F32),
-        pltpu.VMEM((2, NZ, 8, 256), F32),
-        pltpu.VMEM((2, NZ - 1, 8, 256), F32),
-        pltpu.VMEM((2, 2, 256, 256), F32),
+        pltpu.VMEM((2, 2, NY, NX, 64, LANES), F32),
+        pltpu.VMEM((2, 2, NY, NX, 64, LANES), F32),
+        pltpu.VMEM((2, 2, NY, NX, 64, LANES), F32),
+        pltpu.VMEM((2, 2, 3, 4, 64, LANES), F32),
+        pltpu.VMEM((2, 2, 4, 64, LANES), F32),
+        pltpu.VMEM((2, 2, 3, 64, LANES), F32),
+        pltpu.VMEM((2, NZ, 2, 8, LANES), F32),
+        pltpu.VMEM((2, NZ - 1, 2, 8, LANES), F32),
+        pltpu.VMEM((2, 2, NX, NZ, 2, 8, LANES), F32),
         pltpu.VMEM((NLON, 8, LANES), F32),
         pltpu.VMEM((NLON, 8, LANES), F32),
         pltpu.VMEM((8, LANES), F32),
@@ -516,36 +519,29 @@
         pltpu.VMEM((NLON, 8, LANES), F32),
         dma((NCHUNK,)),
         dma,
-        dma((NCHUNK,)),
-        dma((2, 2)),
         dma((7,)), dma((7,)),
         dma((7,)), dma((7,)),
         dma((2,)), dma((2,)),
-        dma((2, 6)), dma((2, 6)),
-        dma((2, 3)), dma((2, 3)),
+        dma((2, 2, 3)), dma((2, 2, 3)),
+        dma((2, 2, 3)), dma((2, 2, 3)),
         dma((2, 7)), dma((2, 7)),
         dma((2, 7)), dma((2, 7)),
-        dma((4,)), dma((4,)),
-        dma((5,)), dma((5,)),
+        dma((2, 2, 3)), dma((2, 2, 3)),
+        dma((2, 2, 4)), dma((2, 2, 4)),
         dma((7,)), dma((7,)),
         dma((7,)), dma((7,)),
         dma((3,)), dma((3,)),
         dma((7,)), dma((7,)),
     ]
-    grad_cells, grad_hidden, grad_out, grad_gain, grad_bias = pl.pallas_call(
+    shapes = (((CELLS, D), BF16), ((D // NY, D), F32), ((80, D), F32), ((1, D), F32), ((1, D), F32))
+    held = pl.pallas_call(
         kernel,
-        out_shape=(
-            jax.ShapeDtypeStruct((CELLS, D), BF16),
-            jax.ShapeDtypeStruct((D // NY, D), F32),
-            jax.ShapeDtypeStruct((D, 80), F32),
-            jax.ShapeDtypeStruct((1, D), F32),
-            jax.ShapeDtypeStruct((1, D), F32),
-        ),
+        out_shape=tuple(pltpu.VMEM(*shape) for shape in shapes),
         in_specs=[hbm, vmem, hbm, vmem, vmem, vmem, vmem, vmem, vmem],
-        out_specs=(hbm, hbm, vmem, vmem, vmem),
+        out_specs=(vmem,) * 5,
         scratch_shapes=scratch,
         compiler_params=pltpu.CompilerParams(
-            collective_id=0, has_side_effects=True, vmem_limit_bytes=60 * 1024 * 1024
+            collective_id=0, has_side_effects=True, vmem_limit_bytes=56 * 1024 * 1024
         ),
         cost_estimate=pl.CostEstimate(flops=10_000_000_000, bytes_accessed=9_000_000, transcendentals=3_000_000),
     )(
@@ -553,16 +549,24 @@
         norm_gain.reshape(1, D),
         hidden_weight,
         hidden_bias.reshape(1, D),
-        output_weight,
+        output_weight.T,
         flux_table,
         target,
         land_sea,
         band_index.reshape(1, ROWS),
     )
+    grad_cells, grad_hidden, grad_out, grad_gain, grad_bias = pl.pallas_call(
+        write_out,
+        out_shape=tuple(jax.ShapeDtypeStruct(*shape) for shape in shapes),
+        in_specs=[vmem] * 5,
+        out_specs=(hbm,) * 5,
+        scratch_shapes=[dma((5,))],
+        compiler_params=pltpu.CompilerParams(vmem_limit_bytes=1024 * 1024),
+    )(*[pltpu.with_memory_space_constraint(array, pltpu.VMEM) for array in held])
     return (
         grad_cells.reshape(latent.shape),
         grad_hidden,
-        grad_out,
+        grad_out.T,
         grad_gain.reshape(D),
         grad_bias.reshape(D),
     )

time: 82.9 us -> 70.8 us (0.85)
  local copies, waits for them, and re-layouts: 9.83 us -> 0 us
  Pallas kernels: 72.2 us -> 69.9 us
    unnamed x12 -> x0, local copies, waits for them, and re-layouts: 9.83 us -> none
    pallas_call x1 -> x2, Pallas kernels: 72.2 us -> 69.9 us  [the longest x1 67.7 us: on_device(): pl.pallas_call(kernel, out_shape=tuple((pltpu.VMEM(*shape) for shape in s...]
where the time goes in v2:
time: 70.8 us; the launch traced here: 70.7 us
  Pallas kernels  69.9 us (99%)
  between operations  0.8 us (1%)
    pallas_call x1, Pallas kernels, on_device(): pl.pallas_call(kernel, out_shape=tuple((pltpu.VMEM(*shape) for shape in s...  67.7 us
    pallas_call x1, Pallas kernels, on_device(): pl.pallas_call(write_out, out_shape=tuple((jax.ShapeDtypeStruct(*shape) f...  2.16 us

profile of v2, /device:TPU:1, one launch (start us, length us, event | category | flops | bytes accessed | tf_op | source)
XLA Modules:
  0.0 70.7 jit_solution(11927663931309059536)
XLA Ops:
  0.6 67.7 %shard_map.128 = (bf16[1536,1024]{1,0:T(8,128)(2,1)S(1)}, f32[256,1024]{1,0:T(8,128)S(1)}, f32[80,1024]{1,0:T(8,128)S(1)}, f32[1,1024]{1,0:T(1,128)S(1)}, f32[1,1024]{1,0:T(1,128)S(1)}) custom-call(bf16[1536,1024]{1,0:T(8,128)(2,1)} %bitcast.9, f32[1,1024]{1,0:T(1,128)} %bitcast.13, bf16[1024,1024]{1,0:T(8,128)(2,1)} %w1_hbm.1, f32[1,1024]{1,0:T(1,128)} %bitcast.14, ...), custom_call_target="tpu_custom_call" | custom-call | flops 10000000000 | bytes 9000000 | tf_op jit(solution)/shard_map/pallas_call | solution.py:537
  68.4 2.2 %shard_map.129 = (bf16[1536,1024]{1,0:T(8,128)(2,1)}, f32[256,1024]{1,0:T(8,128)}, f32[80,1024]{1,0:T(8,128)}, f32[1,1024]{1,0:T(1,128)}, f32[1,1024]{1,0:T(1,128)}) custom-call(bf16[1536,1024]{1,0:T(8,128)(2,1)S(1)} %get-tuple-element.15.refs_0_, f32[256,1024]{1,0:T(8,128)S(1)} %get-tuple-element.16.refs_1_, f32[80,1024]{1,0:T(8,128)S(1)} %get-tuple-element.17.refs_2_, ...), custom_call_target="tpu_custom_call" | custom-call | tf_op jit(solution)/shard_map/pallas_call | solution.py:558

commit v3 on v2

--- a/solution.py
+++ b/solution.py
@@ -35,16 +35,22 @@
     )
 
 
+EARLY = 4
+
+
+def contract(left, right):
+    return lax.dot_general(left, right, (((0,), (0,)), ((), ())), preferred_element_type=F32)
+
+
 def kernel(
-    lat_hbm, gain_ref, w1_hbm, bias_ref, w2_ref, table_ref, target_ref, types_ref, band_ref,
+    lat_hbm, gain_hbm, w1_hbm, bias_hbm, w2_hbm, table_hbm, target_hbm, types_hbm, band_hbm,
     outlat_ref, outhid_ref, outw_ref, outgain_ref, outbias_ref,
-    x_ref, w1_ref, n_ref, nt_ref, v_ref, u_ref, inv_ref, coef_ref, tcol_ref, square_ref,
-    q_ref, tab_ref, s_ref, b_ref, fb_ref, gacc_ref,
-    mine_ref, ex1_ref, line_ref, ex2_ref,
+    x_ref, w1_ref, gain_ref, bias_ref, w2_ref, table_ref, target_ref, types_ref, band_ref,
+    n_ref, v_ref, u_ref, p_ref, inv_ref, coef_ref, tcol_ref, square_ref,
+    q_ref, tab_ref, s_ref, b_ref, fb_ref, gacc_ref, mine_ref, ex_ref,
     give_ref, take_ref, own_ref, first_ref, part_ref, cross_ref, piece_ref, depth_ref,
     hid_ref, sm_ref, sm1_ref, t1_ref, sm2_ref, t2_ref, sm3_ref, smo_ref,
-    xsem, wsem,
-    ex1_s, ex1_r, ex2_s, ex2_r, core_s, core_r, first_s, first_r, cross_s, cross_r, depth_s, depth_r,
+    xsem, wsem, insem, ex_s, ex_r, core_s, core_r, first_s, first_r, cross_s, cross_r, depth_s, depth_r,
     agz_s, agz_r, agx_s, agx_r, agc_s, agc_r, sm1_s, sm1_r, sm2_s, sm2_r, sm3_s, sm3_r, sm4_s, sm4_r,
 ):
     z = lax.axis_index("lat")
@@ -61,19 +67,40 @@
 
     loads = [pltpu.make_async_copy(lat_hbm.at[chunk_rows(i)], x_ref.at[chunk_rows(i)], xsem.at[i]) for i in range(NCHUNK)]
     wload = pltpu.make_async_copy(w1_hbm, w1_ref, wsem)
+    smalls = [
+        pltpu.make_async_copy(source, target, insem.at[i])
+        for i, (source, target) in enumerate(
+            (
+                (w2_hbm, w2_ref),
+                (types_hbm, types_ref),
+                (table_hbm, table_ref),
+                (gain_hbm, gain_ref),
+                (bias_hbm, bias_ref),
+                (band_hbm, band_ref),
+                (target_hbm, target_ref),
+            )
+        )
+    ]
     loads[0].start()
+    for copy in smalls:
+        copy.start()
     wload.start()
     for i in range(1, NCHUNK):
         loads[i].start()
 
     barrier = pltpu.get_barrier_semaphore()
-    for k in range(1, NLON):
-        pl.semaphore_signal(barrier, inc=1, device_id={"lon": lax.rem(lon + k, NLON)}, device_id_type=MESH)
-    for k in range(1, NZ):
-        pl.semaphore_signal(barrier, inc=1, device_id={"lat": lax.rem(z + k, NZ)}, device_id_type=MESH)
+    away = [(dz, dl) for dz in (4, 3, 5, 2, 6, 1, 7, 0) for dl in (4, 5, 3, 2, 6, 7, 1, 0) if (dz, dl) != (0, 0)]
+
+    def over(dz, dl):
+        return {"lat": lax.rem(z + dz, NZ), "lon": lax.rem(lon + dl, NLON)}
+
+    for dz, dl in away:
+        pl.semaphore_signal(barrier, inc=1, device_id=over(dz, dl), device_id_type=MESH)
     for k in range(1, NY):
         pl.semaphore_signal(barrier, inc=1, device_id={"mem": lax.rem(y + k, NY)}, device_id_type=MESH)
 
+    for copy in smalls:
+        copy.wait()
     tab_ref[...] = jnp.zeros_like(tab_ref)
     tab_ref[0:3, :] = table_ref[...]
     table = tab_ref[...]
@@ -142,7 +169,7 @@
     coslat = jnp.where(lane1 < ROWS, coslat, 0.0)
     mine_ref[0:1, :] = coslat * net * (1.0 / (NLON * COLS))
 
-    pl.semaphore_wait(barrier, (NLON - 1) + (NZ - 1) + (NY - 1))
+    pl.semaphore_wait(barrier, len(away) + NY - 1)
     sent = []
 
     def launch(copy):
@@ -150,11 +177,11 @@
         sent.append(copy)
         return copy
 
-    ex1 = [
-        launch(remote(mine_ref, ex1_ref.at[lon], ex1_s.at[k - 1], ex1_r.at[k - 1], lon=lax.rem(lon + k, NLON)))
-        for k in range(1, NLON)
+    ex = [
+        launch(remote(mine_ref, ex_ref.at[z, lon], ex_s.at[dz, dl], ex_r.at[dz, dl], **over(dz, dl)))
+        for dz, dl in away
     ]
-    ex1_ref[lon] = mine_ref[...]
+    ex_ref[z, lon] = mine_ref[...]
 
     def unscaled(i):
         rows = chunk_rows(i)
@@ -177,69 +204,64 @@
         inner = jnp.sum(inner, axis=1, keepdims=True)
         coef_ref[rows, :] = inv * inv * (inner * (1.0 / D))
 
-    def turn(i):
+    def back(i):
         rows = chunk_rows(i)
-        nt_ref[:, rows] = n_ref[rows, :].T
-
-    for i in range(NCHUNK // 2):
+        v_ref[rows, :] = lax.dot_general(
+            u_ref[rows, :], w1_ref[...], (((1,), (1,)), ((), ())), preferred_element_type=F32
+        )
+
+    unscaled(0)
+    for i in range(1, NCHUNK):
+        if i <= EARLY:
+            back(i - 1)
         unscaled(i)
-        turn(i)
-    for copy in ex1:
+    coscol = jnp.sum(jnp.where(diagonal, coslat, 0.0), axis=1, keepdims=True) * (1.0 / (ROWS * NZ))
+    for copy in ex:
         copy.wait_recv()
-    line = ex1_ref[0]
-    for k in range(1, NLON):
-        line = line + ex1_ref[k]
+
+    sums = [jnp.sum(ex_ref[k], axis=0) for k in range(NZ)]
+    weighted = jnp.concatenate([sums[k][0:1, :] for k in range(NZ)], axis=0)
+    targets = jnp.concatenate([ex_ref[k, 0][1:2, :] for k in range(NZ)], axis=0)
     sub8 = lax.broadcasted_iota(jnp.int32, (8, LANES), 0)
-    line_ref[...] = jnp.where(sub8 == 0, line, mine_ref[...])
-    ex2 = [
-        launch(remote(line_ref, ex2_ref.at[z], ex2_s.at[k - 1], ex2_r.at[k - 1], lat=lax.rem(z + k, NZ)))
-        for k in range(1, NZ)
-    ]
-    ex2_ref[z] = line_ref[...]
-    for i in range(NCHUNK // 2, NCHUNK):
-        unscaled(i)
-        turn(i)
-    for copy in ex2:
-        copy.wait_recv()
-
-    lanes8 = lax.broadcasted_iota(jnp.int32, (8, LANES), 1)
-    weighted = jnp.concatenate([ex2_ref[k][0:1, :] for k in range(NZ)], axis=0)
-    targets = jnp.concatenate([ex2_ref[k][1:2, :] for k in range(NZ)], axis=0)
-    above_lane = lax.broadcasted_iota(jnp.int32, (LANES, LANES), 0)
-    here_lane = lax.broadcasted_iota(jnp.int32, (LANES, LANES), 1)
-    upto = (above_lane <= here_lane).astype(F32)
-    local = jnp.dot(weighted, upto, precision=HIGH, preferred_element_type=F32)
-    totals = jnp.sum(weighted, axis=1, keepdims=True)
-    before8 = (lax.broadcasted_iota(jnp.int32, (8, 8), 1) < lax.broadcasted_iota(jnp.int32, (8, 8), 0)).astype(F32)
-    below = jnp.dot(before8, jnp.broadcast_to(totals, (8, LANES)), precision=HIGH, preferred_element_type=F32)
-    misfit = jnp.where(lanes8 < ROWS, local + below - targets, 0.0)
-    onward = (above_lane >= here_lane).astype(F32)
-    from_here = jnp.dot(misfit, onward, precision=HIGH, preferred_element_type=F32)
-    north = jnp.where(sub8 > z, jnp.sum(misfit, axis=1, keepdims=True), jnp.where(sub8 == z, from_here, 0.0))
-    southward = jnp.sum(north, axis=0, keepdims=True)
-    flux = coslat * southward * (1.0 / (ROWS * NZ))
-    flux = jnp.sum(jnp.where(diagonal, flux, 0.0), axis=1, keepdims=True)
+    lane8 = lax.broadcasted_iota(jnp.int32, (8, LANES), 1)
+    count = (ROWS * NZ - ROWS * sub8 - lane8).astype(F32)
+    south = jnp.sum(jnp.where(sub8 < z, weighted, 0.0), axis=0, keepdims=True)
+    north = jnp.sum(jnp.where(sub8 > z, count * weighted - targets, 0.0), axis=0, keepdims=True)
+    here = jnp.sum(jnp.where(sub8 == z, weighted, 0.0), axis=0, keepdims=True)
+    goal = jnp.sum(jnp.where(sub8 == z, targets, 0.0), axis=0, keepdims=True)
+    left_over = ROWS * NZ - ROWS * z
+    both = (left_over - jnp.maximum(subs16, lanes16)).astype(F32) * here
+    both = both + (left_over - subs16).astype(F32) * south + north - jnp.where(lanes16 >= subs16, goal, 0.0)
+    flux = coscol * jnp.sum(both, axis=1, keepdims=True)
     fb_ref[...] = jnp.broadcast_to(flux, (16, LANES))
 
-    for r in range(ROWS):
-        rows = pl.ds(r * COLS, COLS)
-        scale = fb_ref[r : r + 1, 0:1]
-        u_ref[rows, :] = (u_ref[rows, :].astype(F32) * scale).astype(BF16)
-
-    def hidden_tile(ref, half, t):
-        cols = pl.ds(pl.multiple_of(half * 512 + t * 256, 256), 256)
-        tile = jnp.dot(nt_ref[...], u_ref[:, cols], preferred_element_type=F32)
+    def scale_tile(slot, half, t):
+        for way in range(2):
+            cols = pl.ds(pl.multiple_of(half * 512 + t * 256 + way * LANES, LANES), LANES)
+            for r in range(ROWS):
+                rows = pl.ds(r * COLS, COLS)
+                p_ref[slot, rows, way * LANES : (way + 1) * LANES] = (
+                    u_ref[rows, cols].astype(F32) * fb_ref[r : r + 1, :]
+                ).astype(BF16)
+
+    def hidden_tile(ref, slot, t):
+        tile = contract(n_ref[...], p_ref[slot])
         for way in range(2):
             ref[t, way] = tile[:, way * LANES : (way + 1) * LANES].reshape(NY, NX, 64, LANES)
 
     sibling = x * 2 + 1 - core
+    tiles = ((give_ref, 1 - core, 0), (give_ref, 1 - core, 1), (own_ref, core, 0), (own_ref, core, 1))
 
     to_core = []
-    for t in range(2):
-        hidden_tile(give_ref, 1 - core, t)
-        to_core.append(launch(remote(give_ref.at[t], take_ref.at[t], core_s.at[t], core_r.at[t], lon=sibling)))
-    for t in range(2):
-        hidden_tile(own_ref, core, t)
+    scale_tile(0, *tiles[0][1:])
+    for slot in range(4):
+        hidden_tile(tiles[slot][0], slot, tiles[slot][2])
+        if slot < 3:
+            scale_tile(slot + 1, *tiles[slot + 1][1:])
+        if slot < 2:
+            to_core.append(
+                launch(remote(give_ref.at[slot], take_ref.at[slot], core_s.at[slot], core_r.at[slot], lon=sibling))
+            )
 
     def place(way):
         return y if way == 0 else x
@@ -253,11 +275,12 @@
         return own_ref.at[t, way, owner] if way == 0 else own_ref.at[t, way, :, owner]
 
     firsts = {}
-    for t in range(2):
+
+    def first(t):
         to_core[t].wait_recv()
         own_ref[t] = own_ref[t] + take_ref[t]
-        for way in range(2):
-            for k in (2, 1, 3):
+        for k in (2, 1, 3):
+            for way in range(2):
                 firsts[t, way, k] = launch(
                     remote(
                         share(t, way, lax.rem(place(way) + k, 4)),
@@ -268,25 +291,26 @@
                     )
                 )
 
+    first(0)
+
     gacc_ref[...] = jnp.zeros_like(gacc_ref)
 
     def latent_grad(i):
         rows = chunk_rows(i)
-        back = lax.dot_general(
-            u_ref[rows, :], w1_ref[...], (((1,), (1,)), ((), ())), preferred_element_type=F32
+        flux = jnp.concatenate(
+            [jnp.broadcast_to(fb_ref[2 * i + k : 2 * i + k + 1, :], (COLS, LANES)) for k in range(2)], axis=0
         )
-        inv = inv_ref[rows, :]
-        coef = coef_ref[rows, :]
-        coef = jnp.concatenate(
-            [coef[k * COLS : (k + 1) * COLS] * fb_ref[2 * i + k : 2 * i + k + 1, :] for k in range(2)], axis=0
-        )
+        inv = inv_ref[rows, :] * flux
+        coef = coef_ref[rows, :] * flux
         for tile in range(TILES):
             cols = slice(tile * LANES, (tile + 1) * LANES)
             xf = x_ref[rows, cols].astype(F32)
-            scaled = back[:, cols] * inv
+            scaled = v_ref[rows, cols] * inv
             gacc_ref[:, cols] += jnp.sum((scaled * xf).reshape(CHUNK // 8, 8, LANES), axis=0)
             outlat_ref[rows, cols] = (scaled * gain_ref[0:1, cols] - xf * coef).astype(BF16)
 
+    for i in range(EARLY, NCHUNK):
+        back(i)
     for i in range(NCHUNK):
         latent_grad(i)
 
@@ -365,28 +389,24 @@
                 )
             )
 
-    groups = (slice(0, 5), slice(5, 8))
+    groups = (((0, 8),), ((0, 1), (1, 3), (3, 5), (5, 8)))
     agx, agc = {}, {}
 
     def spread(t, g):
-        part = groups[g]
+        start, stop = groups[t][g]
         for k in range(1, NZ):
-            if part.start <= slot_of[NZ - k] < part.stop:
+            if start <= slot_of[NZ - k] < stop:
                 agz[t, k].wait_recv()
-        many = pl.ds(part.start, part.stop - part.start)
-        spot = hid_ref.at[core, t, x, many]
+        spot = hid_ref.at[core, t, x, pl.ds(start, stop - start)]
         for k in (2, 1, 3):
-            agx[t, g, k] = launch(
-                remote(spot, spot, agx_s.at[t, g, k - 1], agx_r.at[t, g, k - 1], lon=lon_at(k))
-            )
+            agx[t, g, k] = launch(remote(spot, spot, agx_s.at[t, g, k - 1], agx_r.at[t, g, k - 1], lon=lon_at(k)))
         agc[t, g, 0] = launch(remote(spot, spot, agc_s.at[t, g, 0], agc_r.at[t, g, 0], lon=sibling))
 
     def to_sibling(t, g):
-        part = groups[g]
-        many = pl.ds(part.start, part.stop - part.start)
+        start, stop = groups[t][g]
         for k in (1, 3, 2):
             agx[t, g, k].wait_recv()
-            spot = hid_ref.at[core, t, lax.rem(x + 4 - k, NX), many]
+            spot = hid_ref.at[core, t, lax.rem(x + 4 - k, NX), pl.ds(start, stop - start)]
             agc[t, g, k] = launch(remote(spot, spot, agc_s.at[t, g, k], agc_r.at[t, g, k], lon=sibling))
 
     def place_rows(half, t):
@@ -397,6 +417,17 @@
                     cols = pl.ds(pl.multiple_of(half * 512 + t * 256 + way * LANES, LANES), LANES)
                     outhid_ref[rows, cols] = hid_ref[half, t, xi, slot_of[k], way]
 
+    def drain(count):
+        for copy in sent[:count]:
+            copy.wait_send()
+        del sent[:count]
+
+    drain(len(ex) + len(to_core))
+    early = [firsts[0, way, k] for way in range(2) for k in range(1, 4)]
+    for copy in early:
+        copy.wait_send()
+    sent[:] = [copy for copy in sent if not any(copy is done for done in early)]
+    first(1)
     cross(0)
     for copy in sm1:
         copy.wait_recv()
@@ -409,8 +440,11 @@
         for k in by_distance
     ]
     sm2_ref[z] = t1_ref[...]
+    drain(len(sm1))
     deepen(0)
     cross(1)
+    drain(len(firsts) // 2 + len(crosses) // 2 + len(sm2))
+    finish(0)
     deepen(1)
     for copy in sm2:
         copy.wait_recv()
@@ -423,7 +457,10 @@
         for k in range(1, NY)
     ]
     sm3_ref[y] = t2_ref[...]
-    finish(0)
+    spread(0, 0)
+    finish(1)
+    spread(1, 0)
+    drain(len(sent) - len(agz) // 2 - 4)
     for copy in sm3:
         copy.wait_recv()
     total = sm3_ref[0]
@@ -434,9 +471,13 @@
         launch(remote(smo_ref.at[lon], smo_ref.at[lon], sm4_s.at[k - 1], sm4_r.at[k - 1], lon=lax.rem(lon + k, NLON)))
         for k in range(1, NLON)
     ]
-    finish(1)
-    spread(0, 0)
-    spread(0, 1)
+    to_sibling(0, 0)
+    place_rows(core, 0)
+    spread(1, 1)
+    to_sibling(1, 0)
+    spread(1, 2)
+    to_sibling(1, 1)
+    spread(1, 3)
     for copy in sm4:
         copy.wait_recv()
     for k in range(NLON):
@@ -446,21 +487,15 @@
         outw_ref[:, cols] = lax.dot_general(
             tab_ref[...], smo_ref[k], (((0,), (0,)), ((), ())), precision=HIGH, preferred_element_type=F32
         )
-    to_sibling(0, 0)
-    to_sibling(0, 1)
-    spread(1, 0)
-    spread(1, 1)
-    place_rows(core, 0)
-    to_sibling(1, 0)
-    to_sibling(1, 1)
-    for g in range(2):
-        for k in range(4):
-            agc[0, g, k].wait_recv()
+    for k in range(4):
+        agc[0, 0, k].wait_recv()
     place_rows(1 - core, 0)
+    drain(len(sent) - 4)
+    to_sibling(1, 2)
+    to_sibling(1, 3)
     place_rows(core, 1)
-    for copy in sent:
-        copy.wait_send()
-    for g in range(2):
+    drain(len(sent))
+    for g in range(4):
         for k in range(4):
             agc[1, g, k].wait_recv()
     place_rows(1 - core, 1)
@@ -483,10 +518,17 @@
     scratch = [
         pltpu.VMEM((CELLS, D), BF16),
         pltpu.VMEM((D, D), BF16),
+        pltpu.VMEM((1, D), F32),
+        pltpu.VMEM((1, D), F32),
+        pltpu.VMEM((80, D), BF16),
+        pltpu.VMEM((3, 80), F32),
+        pltpu.VMEM((1, ROWS), F32),
+        pltpu.VMEM((ROWS, COLS), jnp.int32),
+        pltpu.VMEM((1, ROWS), jnp.int32),
         pltpu.VMEM((CELLS, D), BF16),
-        pltpu.VMEM((D, CELLS), BF16),
         pltpu.VMEM((CELLS, D), F32),
         pltpu.VMEM((CELLS, D), BF16),
+        pltpu.VMEM((4, CELLS, 256), BF16),
         pltpu.VMEM((CELLS, LANES), F32),
         pltpu.VMEM((CELLS, LANES), F32),
         pltpu.VMEM((CELLS, LANES), F32),
@@ -498,9 +540,7 @@
         pltpu.VMEM((16, LANES), F32),
         pltpu.VMEM((8, D), F32),
         pltpu.VMEM((8, LANES), F32),
-        pltpu.VMEM((NLON, 8, LANES), F32),
-        pltpu.VMEM((8, LANES), F32),
-        pltpu.VMEM((NZ, 8, LANES), F32),
+        pltpu.VMEM((NZ, NLON, 8, LANES), F32),
         pltpu.VMEM((2, 2, NY, NX, 64, LANES), F32),
         pltpu.VMEM((2, 2, NY, NX, 64, LANES), F32),
         pltpu.VMEM((2, 2, NY, NX, 64, LANES), F32),
@@ -519,15 +559,15 @@
         pltpu.VMEM((NLON, 8, LANES), F32),
         dma((NCHUNK,)),
         dma,
-        dma((7,)), dma((7,)),
-        dma((7,)), dma((7,)),
+        dma((7,)),
+        dma((NZ, NLON)), dma((NZ, NLON)),
         dma((2,)), dma((2,)),
         dma((2, 2, 3)), dma((2, 2, 3)),
         dma((2, 2, 3)), dma((2, 2, 3)),
         dma((2, 7)), dma((2, 7)),
         dma((2, 7)), dma((2, 7)),
-        dma((2, 2, 3)), dma((2, 2, 3)),
-        dma((2, 2, 4)), dma((2, 2, 4)),
+        dma((2, 4, 3)), dma((2, 4, 3)),
+        dma((2, 4, 4)), dma((2, 4, 4)),
         dma((7,)), dma((7,)),
         dma((7,)), dma((7,)),
         dma((3,)), dma((3,)),
@@ -537,7 +577,7 @@
     held = pl.pallas_call(
         kernel,
         out_shape=tuple(pltpu.VMEM(*shape) for shape in shapes),
-        in_specs=[hbm, vmem, hbm, vmem, vmem, vmem, vmem, vmem, vmem],
+        in_specs=[hbm] * 9,
         out_specs=(vmem,) * 5,
         scratch_shapes=scratch,
         compiler_params=pltpu.CompilerParams(

time: 70.8 us -> 77 us (1.088)
  Pallas kernels: 69.9 us -> 76.1 us
    pallas_call x1, Pallas kernels: 67.7 us -> 73.9 us  [on_device(): pl.pallas_call(kernel, out_shape=tuple((pltpu.VMEM(*shape) for shape in s...]
where the time goes in v3:
time: 77 us; the launch traced here: 76.9 us
  Pallas kernels  76.1 us (99%)
  between operations  0.8 us (1%)
    pallas_call x1, Pallas kernels, on_device(): pl.pallas_call(kernel, out_shape=tuple((pltpu.VMEM(*shape) for shape in s...  73.9 us
    pallas_call x1, Pallas kernels, on_device(): pl.pallas_call(write_out, out_shape=tuple((jax.ShapeDtypeStruct(*shape) f...  2.16 us

profile of v3, /device:TPU:1, one launch (start us, length us, event | category | flops | bytes accessed | tf_op | source)
XLA Modules:
  0.0 76.9 jit_solution(16151756861902625767)
XLA Ops:
  0.6 73.9 %shard_map.128 = (bf16[1536,1024]{1,0:T(8,128)(2,1)S(1)}, f32[256,1024]{1,0:T(8,128)S(1)}, f32[80,1024]{1,0:T(8,128)S(1)}, f32[1,1024]{1,0:T(1,128)S(1)}, f32[1,1024]{1,0:T(1,128)S(1)}) custom-call(bf16[1536,1024]{1,0:T(8,128)(2,1)} %bitcast.9, f32[1,1024]{1,0:T(1,128)} %bitcast.13, bf16[1024,1024]{1,0:T(8,128)(2,1)} %w1_hbm.1, f32[1,1024]{1,0:T(1,128)} %bitcast.14, ...), custom_call_target="tpu_custom_call" | custom-call | flops 10000000000 | bytes 9000000 | tf_op jit(solution)/shard_map/pallas_call | solution.py:577
  74.6 2.2 %shard_map.129 = (bf16[1536,1024]{1,0:T(8,128)(2,1)}, f32[256,1024]{1,0:T(8,128)}, f32[80,1024]{1,0:T(8,128)}, f32[1,1024]{1,0:T(1,128)}, f32[1,1024]{1,0:T(1,128)}) custom-call(bf16[1536,1024]{1,0:T(8,128)(2,1)S(1)} %get-tuple-element.15.refs_0_, f32[256,1024]{1,0:T(8,128)S(1)} %get-tuple-element.16.refs_1_, f32[80,1024]{1,0:T(8,128)S(1)} %get-tuple-element.17.refs_2_, ...), custom_call_target="tpu_custom_call" | custom-call | tf_op jit(solution)/shard_map/pallas_call | solution.py:598

commit v4 on v3

--- a/solution.py
+++ b/solution.py
@@ -35,9 +35,6 @@
     )
 
 
-EARLY = 4
-
-
 def contract(left, right):
     return lax.dot_general(left, right, (((0,), (0,)), ((), ())), preferred_element_type=F32)
 
@@ -47,10 +44,10 @@
     outlat_ref, outhid_ref, outw_ref, outgain_ref, outbias_ref,
     x_ref, w1_ref, gain_ref, bias_ref, w2_ref, table_ref, target_ref, types_ref, band_ref,
     n_ref, v_ref, u_ref, p_ref, inv_ref, coef_ref, tcol_ref, square_ref,
-    q_ref, tab_ref, s_ref, b_ref, fb_ref, gacc_ref, mine_ref, ex_ref,
+    q_ref, tab_ref, s_ref, b_ref, fb_ref, gacc_ref, mine_ref, ex1_ref, line_ref, ex2_ref,
     give_ref, take_ref, own_ref, first_ref, part_ref, cross_ref, piece_ref, depth_ref,
     hid_ref, sm_ref, sm1_ref, t1_ref, sm2_ref, t2_ref, sm3_ref, smo_ref,
-    xsem, wsem, insem, ex_s, ex_r, core_s, core_r, first_s, first_r, cross_s, cross_r, depth_s, depth_r,
+    xsem, wsem, insem, ex1_s, ex1_r, ex2_s, ex2_r, core_s, core_r, first_s, first_r, cross_s, cross_r, depth_s, depth_r,
     agz_s, agz_r, agx_s, agx_r, agc_s, agc_r, sm1_s, sm1_r, sm2_s, sm2_r, sm3_s, sm3_r, sm4_s, sm4_r,
 ):
     z = lax.axis_index("lat")
@@ -89,13 +86,10 @@
         loads[i].start()
 
     barrier = pltpu.get_barrier_semaphore()
-    away = [(dz, dl) for dz in (4, 3, 5, 2, 6, 1, 7, 0) for dl in (4, 5, 3, 2, 6, 7, 1, 0) if (dz, dl) != (0, 0)]
-
-    def over(dz, dl):
-        return {"lat": lax.rem(z + dz, NZ), "lon": lax.rem(lon + dl, NLON)}
-
-    for dz, dl in away:
-        pl.semaphore_signal(barrier, inc=1, device_id=over(dz, dl), device_id_type=MESH)
+    for k in range(1, NLON):
+        pl.semaphore_signal(barrier, inc=1, device_id={"lon": lax.rem(lon + k, NLON)}, device_id_type=MESH)
+    for k in range(1, NZ):
+        pl.semaphore_signal(barrier, inc=1, device_id={"lat": lax.rem(z + k, NZ)}, device_id_type=MESH)
     for k in range(1, NY):
         pl.semaphore_signal(barrier, inc=1, device_id={"mem": lax.rem(y + k, NY)}, device_id_type=MESH)
 
@@ -169,7 +163,7 @@
     coslat = jnp.where(lane1 < ROWS, coslat, 0.0)
     mine_ref[0:1, :] = coslat * net * (1.0 / (NLON * COLS))
 
-    pl.semaphore_wait(barrier, len(away) + NY - 1)
+    pl.semaphore_wait(barrier, (NLON - 1) + (NZ - 1) + (NY - 1))
     sent = []
 
     def launch(copy):
@@ -177,11 +171,12 @@
         sent.append(copy)
         return copy
 
-    ex = [
-        launch(remote(mine_ref, ex_ref.at[z, lon], ex_s.at[dz, dl], ex_r.at[dz, dl], **over(dz, dl)))
-        for dz, dl in away
+    by_distance = (4, 3, 5, 2, 6, 1, 7)
+    ex1 = [
+        launch(remote(mine_ref, ex1_ref.at[lon], ex1_s.at[k - 1], ex1_r.at[k - 1], lon=lax.rem(lon + k, NLON)))
+        for k in by_distance
     ]
-    ex_ref[z, lon] = mine_ref[...]
+    ex1_ref[lon] = mine_ref[...]
 
     def unscaled(i):
         rows = chunk_rows(i)
@@ -210,20 +205,30 @@
             u_ref[rows, :], w1_ref[...], (((1,), (1,)), ((), ())), preferred_element_type=F32
         )
 
-    unscaled(0)
-    for i in range(1, NCHUNK):
-        if i <= EARLY:
+    for i in range(NCHUNK // 2):
+        unscaled(i)
+        if i >= 1:
             back(i - 1)
-        unscaled(i)
     coscol = jnp.sum(jnp.where(diagonal, coslat, 0.0), axis=1, keepdims=True) * (1.0 / (ROWS * NZ))
-    for copy in ex:
+    for copy in ex1:
         copy.wait_recv()
-
-    sums = [jnp.sum(ex_ref[k], axis=0) for k in range(NZ)]
-    weighted = jnp.concatenate([sums[k][0:1, :] for k in range(NZ)], axis=0)
-    targets = jnp.concatenate([ex_ref[k, 0][1:2, :] for k in range(NZ)], axis=0)
     sub8 = lax.broadcasted_iota(jnp.int32, (8, LANES), 0)
     lane8 = lax.broadcasted_iota(jnp.int32, (8, LANES), 1)
+    line_ref[...] = jnp.where(sub8 == 0, jnp.sum(ex1_ref[...], axis=0), mine_ref[...])
+    ex2 = [
+        launch(remote(line_ref, ex2_ref.at[z], ex2_s.at[k - 1], ex2_r.at[k - 1], lat=lax.rem(z + k, NZ)))
+        for k in by_distance
+    ]
+    ex2_ref[z] = line_ref[...]
+    for i in range(NCHUNK // 2, NCHUNK):
+        unscaled(i)
+        back(i - 1)
+    back(NCHUNK - 1)
+    for copy in ex2:
+        copy.wait_recv()
+
+    weighted = jnp.concatenate([ex2_ref[k][0:1, :] for k in range(NZ)], axis=0)
+    targets = jnp.concatenate([ex2_ref[k][1:2, :] for k in range(NZ)], axis=0)
     count = (ROWS * NZ - ROWS * sub8 - lane8).astype(F32)
     south = jnp.sum(jnp.where(sub8 < z, weighted, 0.0), axis=0, keepdims=True)
     north = jnp.sum(jnp.where(sub8 > z, count * weighted - targets, 0.0), axis=0, keepdims=True)
@@ -250,18 +255,7 @@
             ref[t, way] = tile[:, way * LANES : (way + 1) * LANES].reshape(NY, NX, 64, LANES)
 
     sibling = x * 2 + 1 - core
-    tiles = ((give_ref, 1 - core, 0), (give_ref, 1 - core, 1), (own_ref, core, 0), (own_ref, core, 1))
-
-    to_core = []
-    scale_tile(0, *tiles[0][1:])
-    for slot in range(4):
-        hidden_tile(tiles[slot][0], slot, tiles[slot][2])
-        if slot < 3:
-            scale_tile(slot + 1, *tiles[slot + 1][1:])
-        if slot < 2:
-            to_core.append(
-                launch(remote(give_ref.at[slot], take_ref.at[slot], core_s.at[slot], core_r.at[slot], lon=sibling))
-            )
+    tiles = ((give_ref, 1 - core, 0), (own_ref, core, 0), (give_ref, 1 - core, 1), (own_ref, core, 1))
 
     def place(way):
         return y if way == 0 else x
@@ -291,7 +285,20 @@
                     )
                 )
 
-    first(0)
+    to_core = []
+    scale_tile(0, *tiles[0][1:])
+    for slot in range(4):
+        ref, _, t = tiles[slot]
+        hidden_tile(ref, slot, t)
+        if ref is give_ref:
+            to_core.append(
+                launch(remote(give_ref.at[t], take_ref.at[t], core_s.at[t], core_r.at[t], lon=sibling))
+            )
+        if slot < 3:
+            scale_tile(slot + 1, *tiles[slot + 1][1:])
+        if slot == 2:
+            first(0)
+    first(1)
 
     gacc_ref[...] = jnp.zeros_like(gacc_ref)
 
@@ -309,8 +316,6 @@
             gacc_ref[:, cols] += jnp.sum((scaled * xf).reshape(CHUNK // 8, 8, LANES), axis=0)
             outlat_ref[rows, cols] = (scaled * gain_ref[0:1, cols] - xf * coef).astype(BF16)
 
-    for i in range(EARLY, NCHUNK):
-        back(i)
     for i in range(NCHUNK):
         latent_grad(i)
 
@@ -352,8 +357,6 @@
                     )
                 )
 
-    by_distance = (4, 3, 5, 2, 6, 1, 7)
-
     def deepen(t):
         for way in range(2):
             for k in range(1, 4):
@@ -389,7 +392,7 @@
                 )
             )
 
-    groups = (((0, 8),), ((0, 1), (1, 3), (3, 5), (5, 8)))
+    groups = (((0, 5), (5, 8)), ((0, 5), (5, 8)))
     agx, agc = {}, {}
 
     def spread(t, g):
@@ -422,80 +425,65 @@
             copy.wait_send()
         del sent[:count]
 
-    drain(len(ex) + len(to_core))
-    early = [firsts[0, way, k] for way in range(2) for k in range(1, 4)]
-    for copy in early:
-        copy.wait_send()
-    sent[:] = [copy for copy in sent if not any(copy is done for done in early)]
-    first(1)
-    cross(0)
+    drain(len(ex1) + len(ex2) + len(to_core))
     for copy in sm1:
         copy.wait_recv()
-    total = sm1_ref[0]
-    for k in range(1, NLON):
-        total = total + sm1_ref[k]
-    t1_ref[...] = total
+    t1_ref[...] = jnp.sum(sm1_ref[...], axis=0)
     sm2 = [
         launch(remote(t1_ref, sm2_ref.at[z], sm2_s.at[k - 1], sm2_r.at[k - 1], lat=lax.rem(z + k, NZ)))
         for k in by_distance
     ]
     sm2_ref[z] = t1_ref[...]
-    drain(len(sm1))
-    deepen(0)
+    cross(0)
     cross(1)
-    drain(len(firsts) // 2 + len(crosses) // 2 + len(sm2))
-    finish(0)
-    deepen(1)
+    drain(len(firsts) + len(sm1))
     for copy in sm2:
         copy.wait_recv()
-    total = sm2_ref[0]
-    for k in range(1, NZ):
-        total = total + sm2_ref[k]
-    t2_ref[...] = total
+    t2_ref[...] = jnp.sum(sm2_ref[...], axis=0)
     sm3 = [
         launch(remote(t2_ref, sm3_ref.at[y], sm3_s.at[k - 1], sm3_r.at[k - 1], mem=lax.rem(y + k, NY)))
         for k in range(1, NY)
     ]
     sm3_ref[y] = t2_ref[...]
-    spread(0, 0)
-    finish(1)
-    spread(1, 0)
-    drain(len(sent) - len(agz) // 2 - 4)
+    deepen(0)
+    deepen(1)
+    drain(len(sm2) + len(crosses))
     for copy in sm3:
         copy.wait_recv()
-    total = sm3_ref[0]
-    for k in range(1, NY):
-        total = total + sm3_ref[k]
-    smo_ref[lon] = total
+    smo_ref[lon] = jnp.sum(sm3_ref[...], axis=0)
     sm4 = [
         launch(remote(smo_ref.at[lon], smo_ref.at[lon], sm4_s.at[k - 1], sm4_r.at[k - 1], lon=lax.rem(lon + k, NLON)))
-        for k in range(1, NLON)
+        for k in by_distance
     ]
-    to_sibling(0, 0)
-    place_rows(core, 0)
-    spread(1, 1)
-    to_sibling(1, 0)
-    spread(1, 2)
-    to_sibling(1, 1)
-    spread(1, 3)
+    finish(0)
+    finish(1)
+    drain(len(sm3) + len(depths))
     for copy in sm4:
         copy.wait_recv()
-    for k in range(NLON):
-        cols = slice(k * LANES, (k + 1) * LANES)
-        outbias_ref[0:1, cols] = smo_ref[k][3:4, :]
-        outgain_ref[0:1, cols] = smo_ref[k][4:5, :]
-        outw_ref[:, cols] = lax.dot_general(
-            tab_ref[...], smo_ref[k], (((0,), (0,)), ((), ())), precision=HIGH, preferred_element_type=F32
-        )
-    for k in range(4):
-        agc[0, 0, k].wait_recv()
+    summed = jnp.concatenate([smo_ref[k] for k in range(NLON)], axis=1)
+    outbias_ref[...] = summed[3:4, :]
+    outgain_ref[...] = summed[4:5, :]
+    outw_ref[...] = lax.dot_general(
+        tab_ref[...], summed, (((0,), (0,)), ((), ())), precision=HIGH, preferred_element_type=F32
+    )
+    spread(0, 0)
+    spread(0, 1)
+    spread(1, 0)
+    spread(1, 1)
+    drain(len(sm4) + len(agz))
+    to_sibling(0, 0)
+    to_sibling(0, 1)
+    place_rows(core, 0)
+    to_sibling(1, 0)
+    to_sibling(1, 1)
+    place_rows(core, 1)
+    drain(len(agx))
+    for g in range(2):
+        for k in range(4):
+            agc[0, g, k].wait_recv()
     place_rows(1 - core, 0)
-    drain(len(sent) - 4)
-    to_sibling(1, 2)
-    to_sibling(1, 3)
-    place_rows(core, 1)
     drain(len(sent))
-    for g in range(4):
+    for g in range(2):
         for k in range(4):
             agc[1, g, k].wait_recv()
     place_rows(1 - core, 1)
@@ -540,7 +528,9 @@
         pltpu.VMEM((16, LANES), F32),
         pltpu.VMEM((8, D), F32),
         pltpu.VMEM((8, LANES), F32),
-        pltpu.VMEM((NZ, NLON, 8, LANES), F32),
+        pltpu.VMEM((NLON, 8, LANES), F32),
+        pltpu.VMEM((8, LANES), F32),
+        pltpu.VMEM((NZ, 8, LANES), F32),
         pltpu.VMEM((2, 2, NY, NX, 64, LANES), F32),
         pltpu.VMEM((2, 2, NY, NX, 64, LANES), F32),
         pltpu.VMEM((2, 2, NY, NX, 64, LANES), F32),
@@ -560,14 +550,15 @@
         dma((NCHUNK,)),
         dma,
         dma((7,)),
-        dma((NZ, NLON)), dma((NZ, NLON)),
+        dma((7,)), dma((7,)),
+        dma((7,)), dma((7,)),
         dma((2,)), dma((2,)),
         dma((2, 2, 3)), dma((2, 2, 3)),
         dma((2, 2, 3)), dma((2, 2, 3)),
         dma((2, 7)), dma((2, 7)),
         dma((2, 7)), dma((2, 7)),
-        dma((2, 4, 3)), dma((2, 4, 3)),
-        dma((2, 4, 4)), dma((2, 4, 4)),
+        dma((2, 2, 3)), dma((2, 2, 3)),
+        dma((2, 2, 4)), dma((2, 2, 4)),
         dma((7,)), dma((7,)),
         dma((7,)), dma((7,)),
         dma((3,)), dma((3,)),

time: 77 us -> 69.6 us (0.904)
  Pallas kernels: 76.1 us -> 68.8 us
    pallas_call x1, Pallas kernels: 73.9 us -> 66.6 us  [on_device(): pl.pallas_call(kernel, out_shape=tuple((pltpu.VMEM(*shape) for shape in s...]
where the time goes in v4:
time: 69.6 us
  Pallas kernels  68.8 us (99%)
  between operations  0.8 us (1%)
    pallas_call x1, Pallas kernels, on_device(): pl.pallas_call(kernel, out_shape=tuple((pltpu.VMEM(*shape) for shape in s...  66.6 us
    pallas_call x1, Pallas kernels, on_device(): pl.pallas_call(write_out, out_shape=tuple((jax.ShapeDtypeStruct(*shape) f...  2.16 us

profile of v4, /device:TPU:1, one launch (start us, length us, event | category | flops | bytes accessed | tf_op | source)
XLA Modules:
  0.0 69.6 jit_solution(1038609077263909088)
XLA Ops:
  0.6 66.6 %shard_map.128 = (bf16[1536,1024]{1,0:T(8,128)(2,1)S(1)}, f32[256,1024]{1,0:T(8,128)S(1)}, f32[80,1024]{1,0:T(8,128)S(1)}, f32[1,1024]{1,0:T(1,128)S(1)}, f32[1,1024]{1,0:T(1,128)S(1)}) custom-call(bf16[1536,1024]{1,0:T(8,128)(2,1)} %bitcast.9, f32[1,1024]{1,0:T(1,128)} %bitcast.13, bf16[1024,1024]{1,0:T(8,128)(2,1)} %w1_hbm.1, f32[1,1024]{1,0:T(1,128)} %bitcast.14, ...), custom_call_target="tpu_custom_call" | custom-call | flops 10000000000 | bytes 9000000 | tf_op jit(solution)/shard_map/pallas_call | solution.py:568
  67.2 2.2 %shard_map.129 = (bf16[1536,1024]{1,0:T(8,128)(2,1)}, f32[256,1024]{1,0:T(8,128)}, f32[80,1024]{1,0:T(8,128)}, f32[1,1024]{1,0:T(1,128)}, f32[1,1024]{1,0:T(1,128)}) custom-call(bf16[1536,1024]{1,0:T(8,128)(2,1)S(1)} %get-tuple-element.15.refs_0_, f32[256,1024]{1,0:T(8,128)S(1)} %get-tuple-element.16.refs_1_, f32[80,1024]{1,0:T(8,128)S(1)} %get-tuple-element.17.refs_2_, ...), custom_call_target="tpu_custom_call" | custom-call | tf_op jit(solution)/shard_map/pallas_call | solution.py:589

commit v5 on v4

--- a/solution.py
+++ b/solution.py
@@ -45,7 +45,7 @@
     x_ref, w1_ref, gain_ref, bias_ref, w2_ref, table_ref, target_ref, types_ref, band_ref,
     n_ref, v_ref, u_ref, p_ref, inv_ref, coef_ref, tcol_ref, square_ref,
     q_ref, tab_ref, s_ref, b_ref, fb_ref, gacc_ref, mine_ref, ex1_ref, line_ref, ex2_ref,
-    give_ref, take_ref, own_ref, first_ref, part_ref, cross_ref, piece_ref, depth_ref,
+    give_ref, take_ref, own_ref, pass_ref, plain_ref, agg_ref, part_ref, cross_ref, piece_ref, depth_ref,
     hid_ref, sm_ref, sm1_ref, t1_ref, sm2_ref, t2_ref, sm3_ref, smo_ref,
     xsem, wsem, insem, ex1_s, ex1_r, ex2_s, ex2_r, core_s, core_r, first_s, first_r, cross_s, cross_r, depth_s, depth_r,
     agz_s, agz_r, agx_s, agx_r, agc_s, agc_r, sm1_s, sm1_r, sm2_s, sm2_r, sm3_s, sm3_r, sm4_s, sm4_r,
@@ -63,7 +63,9 @@
         return pl.ds(i * CHUNK, CHUNK)
 
     loads = [pltpu.make_async_copy(lat_hbm.at[chunk_rows(i)], x_ref.at[chunk_rows(i)], xsem.at[i]) for i in range(NCHUNK)]
-    wload = pltpu.make_async_copy(w1_hbm, w1_ref, wsem)
+    wloads = [
+        pltpu.make_async_copy(w1_hbm.at[pl.ds(i * 256, 256)], w1_ref.at[pl.ds(i * 256, 256)], wsem.at[i]) for i in range(4)
+    ]
     smalls = [
         pltpu.make_async_copy(source, target, insem.at[i])
         for i, (source, target) in enumerate(
@@ -81,7 +83,8 @@
     loads[0].start()
     for copy in smalls:
         copy.start()
-    wload.start()
+    for copy in wloads:
+        copy.start()
     for i in range(1, NCHUNK):
         loads[i].start()
 
@@ -93,25 +96,26 @@
     for k in range(1, NY):
         pl.semaphore_signal(barrier, inc=1, device_id={"mem": lax.rem(y + k, NY)}, device_id_type=MESH)
 
+    def tables():
+        tab_ref[...] = jnp.zeros_like(tab_ref)
+        tab_ref[0:3, :] = table_ref[...]
+        table = tab_ref[...]
+        high = table.astype(BF16)
+        rest = table - high.astype(F32)
+        middle = rest.astype(BF16)
+        w2 = w2_ref[...]
+        dims = (((1,), (0,)), ((), ()))
+        q_ref[...] = lax.dot_general(high, w2, dims, preferred_element_type=F32) + lax.dot_general(
+            middle, w2, dims, preferred_element_type=F32
+        )
+        square_ref[...] = jnp.zeros_like(square_ref)
+        square_ref[0:ROWS, :] = types_ref[...].astype(F32)
+        turned = square_ref[...].T
+        for r in range(ROWS):
+            tcol_ref[r * COLS : (r + 1) * COLS, :] = jnp.broadcast_to(turned[:, r : r + 1], (COLS, LANES))
+
     for copy in smalls:
         copy.wait()
-    tab_ref[...] = jnp.zeros_like(tab_ref)
-    tab_ref[0:3, :] = table_ref[...]
-    table = tab_ref[...]
-    high = table.astype(BF16)
-    rest = table - high.astype(F32)
-    middle = rest.astype(BF16)
-    w2 = w2_ref[...]
-    dims = (((1,), (0,)), ((), ()))
-    q_ref[...] = lax.dot_general(high, w2, dims, preferred_element_type=F32) + lax.dot_general(
-        middle, w2, dims, preferred_element_type=F32
-    )
-    square_ref[...] = jnp.zeros_like(square_ref)
-    square_ref[0:ROWS, :] = types_ref[...].astype(F32)
-    turned = square_ref[...].T
-    for r in range(ROWS):
-        tcol_ref[r * COLS : (r + 1) * COLS, :] = jnp.broadcast_to(turned[:, r : r + 1], (COLS, LANES))
-
     gain = gain_ref[...]
     bias = bias_ref[...]
 
@@ -139,11 +143,14 @@
         s_ref[i * 16 : (i + 1) * 16, :] = jnp.dot(onehot, act, preferred_element_type=F32)
 
     normalise(0)
-    wload.wait()
+    for copy in wloads:
+        copy.wait()
     for i in range(NCHUNK):
         first_dot(i)
         if i + 1 < NCHUNK:
             normalise(i + 1)
+        if i == 0:
+            tables()
         if i >= 1:
             activate(i - 1)
     activate(NCHUNK - 1)
@@ -265,25 +272,42 @@
             return {"mem": lax.rem(y + step, NY)}
         return {"lon": lon_at(step)}
 
-    def share(t, way, owner):
-        return own_ref.at[t, way, owner] if way == 0 else own_ref.at[t, way, :, owner]
-
-    firsts = {}
+    def half(t, way, owner, which):
+        rows = pl.ds(32 * which, 32)
+        return own_ref.at[t, way, owner, :, rows] if way == 0 else own_ref.at[t, way, :, owner, rows]
+
+    passes, plains, aggs = {}, {}, {}
+
+    def hop(table, t, way, which, step, owner, target, sem):
+        table[t, way, which] = launch(
+            remote(
+                half(t, way, owner, which),
+                target.at[t, way, which],
+                first_s.at[t, way, sem],
+                first_r.at[t, way, sem],
+                **toward(way, step),
+            )
+        )
 
     def first(t):
         to_core[t].wait_recv()
         own_ref[t] = own_ref[t] + take_ref[t]
-        for k in (2, 1, 3):
-            for way in range(2):
-                firsts[t, way, k] = launch(
-                    remote(
-                        share(t, way, lax.rem(place(way) + k, 4)),
-                        first_ref.at[t, way, k - 1],
-                        first_s.at[t, way, k - 1],
-                        first_r.at[t, way, k - 1],
-                        **toward(way, k),
-                    )
-                )
+        for way in range(2):
+            opposite = lax.rem(place(way) + 2, 4)
+            hop(passes, t, way, 0, 1, opposite, pass_ref, 0)
+            hop(passes, t, way, 1, 3, opposite, pass_ref, 1)
+        for way in range(2):
+            hop(plains, t, way, 1, 1, lax.rem(place(way) + 1, 4), plain_ref, 2)
+            hop(plains, t, way, 0, 3, lax.rem(place(way) + 3, 4), plain_ref, 3)
+
+    def ring(t):
+        for way in range(2):
+            for which, step in ((0, 1), (1, 3)):
+                owner = lax.rem(place(way) + step, 4)
+                passes[t, way, which].wait_recv()
+                mid = half(t, way, owner, which)
+                mid[...] = mid[...] + pass_ref[t, way, which]
+                hop(aggs, t, way, which, step, owner, agg_ref, 4 + which)
 
     to_core = []
     scale_tile(0, *tiles[0][1:])
@@ -297,6 +321,7 @@
         if slot < 3:
             scale_tile(slot + 1, *tiles[slot + 1][1:])
         if slot == 2:
+            pass
             first(0)
     first(1)
 
@@ -340,11 +365,12 @@
 
     def cross(t):
         for way in range(2):
-            for k in range(1, 4):
-                firsts[t, way, k].wait_recv()
-            part_ref[t, way] = (
-                share(t, way, place(way))[...] + first_ref[t, way, 0] + first_ref[t, way, 1] + first_ref[t, way, 2]
-            )
+            for which in range(2):
+                plains[t, way, which].wait_recv()
+                aggs[t, way, which].wait_recv()
+                part_ref[t, way, :, 32 * which : 32 * (which + 1)] = (
+                    half(t, way, place(way), which)[...] + plain_ref[t, way, which] + agg_ref[t, way, which]
+                )
             other = 1 - way
             for k in (2, 1, 3):
                 crosses[t, way, k] = launch(
@@ -425,7 +451,11 @@
             copy.wait_send()
         del sent[:count]
 
+    ring(0)
+    ring(1)
     drain(len(ex1) + len(ex2) + len(to_core))
+    cross(0)
+    cross(1)
     for copy in sm1:
         copy.wait_recv()
     t1_ref[...] = jnp.sum(sm1_ref[...], axis=0)
@@ -434,9 +464,9 @@
         for k in by_distance
     ]
     sm2_ref[z] = t1_ref[...]
-    cross(0)
-    cross(1)
-    drain(len(firsts) + len(sm1))
+    drain(len(passes) + len(plains) + len(sm1) + len(aggs))
+    deepen(0)
+    deepen(1)
     for copy in sm2:
         copy.wait_recv()
     t2_ref[...] = jnp.sum(sm2_ref[...], axis=0)
@@ -445,9 +475,9 @@
         for k in range(1, NY)
     ]
     sm3_ref[y] = t2_ref[...]
-    deepen(0)
-    deepen(1)
-    drain(len(sm2) + len(crosses))
+    drain(len(crosses) + len(sm2))
+    finish(0)
+    finish(1)
     for copy in sm3:
         copy.wait_recv()
     smo_ref[lon] = jnp.sum(sm3_ref[...], axis=0)
@@ -455,9 +485,11 @@
         launch(remote(smo_ref.at[lon], smo_ref.at[lon], sm4_s.at[k - 1], sm4_r.at[k - 1], lon=lax.rem(lon + k, NLON)))
         for k in by_distance
     ]
-    finish(0)
-    finish(1)
-    drain(len(sm3) + len(depths))
+    drain(len(depths) + len(sm3))
+    spread(0, 0)
+    spread(0, 1)
+    spread(1, 0)
+    spread(1, 1)
     for copy in sm4:
         copy.wait_recv()
     summed = jnp.concatenate([smo_ref[k] for k in range(NLON)], axis=1)
@@ -466,11 +498,7 @@
     outw_ref[...] = lax.dot_general(
         tab_ref[...], summed, (((0,), (0,)), ((), ())), precision=HIGH, preferred_element_type=F32
     )
-    spread(0, 0)
-    spread(0, 1)
-    spread(1, 0)
-    spread(1, 1)
-    drain(len(sm4) + len(agz))
+    drain(len(agz) + len(sm4))
     to_sibling(0, 0)
     to_sibling(0, 1)
     place_rows(core, 0)
@@ -492,7 +520,16 @@
 def write_out(*refs):
     sems = refs[-1]
     half = len(refs) // 2
-    copies = [pltpu.make_async_copy(refs[i], refs[half + i], sems.at[i]) for i in range(half)]
+    copies = []
+    for source, target in zip(refs[:half], refs[half:-1]):
+        rows = source.shape[0]
+        step = min(rows, 256 if source.dtype == BF16 else 64)
+        for start in range(0, rows - rows % step, step):
+            part = pl.ds(start, step) if step < rows else slice(None)
+            copies.append(pltpu.make_async_copy(source.at[part], target.at[part], sems.at[len(copies)]))
+        if rows % step:
+            part = pl.ds(rows - rows % step, rows % step)
+            copies.append(pltpu.make_async_copy(source.at[part], target.at[part], sems.at[len(copies)]))
     for copy in copies:
         copy.start()
     for copy in copies:
@@ -534,7 +571,9 @@
         pltpu.VMEM((2, 2, NY, NX, 64, LANES), F32),
         pltpu.VMEM((2, 2, NY, NX, 64, LANES), F32),
         pltpu.VMEM((2, 2, NY, NX, 64, LANES), F32),
-        pltpu.VMEM((2, 2, 3, 4, 64, LANES), F32),
+        pltpu.VMEM((2, 2, 2, 4, 32, LANES), F32),
+        pltpu.VMEM((2, 2, 2, 4, 32, LANES), F32),
+        pltpu.VMEM((2, 2, 2, 4, 32, LANES), F32),
         pltpu.VMEM((2, 2, 4, 64, LANES), F32),
         pltpu.VMEM((2, 2, 3, 64, LANES), F32),
         pltpu.VMEM((2, NZ, 2, 8, LANES), F32),
@@ -548,12 +587,12 @@
         pltpu.VMEM((NY, 8, LANES), F32),
         pltpu.VMEM((NLON, 8, LANES), F32),
         dma((NCHUNK,)),
-        dma,
+        dma((4,)),
         dma((7,)),
         dma((7,)), dma((7,)),
         dma((7,)), dma((7,)),
         dma((2,)), dma((2,)),
-        dma((2, 2, 3)), dma((2, 2, 3)),
+        dma((2, 2, 6)), dma((2, 2, 6)),
         dma((2, 2, 3)), dma((2, 2, 3)),
         dma((2, 7)), dma((2, 7)),
         dma((2, 7)), dma((2, 7)),
@@ -591,7 +630,7 @@
         out_shape=tuple(jax.ShapeDtypeStruct(*shape) for shape in shapes),
         in_specs=[vmem] * 5,
         out_specs=(hbm,) * 5,
-        scratch_shapes=[dma((5,))],
+        scratch_shapes=[dma((16,))],
         compiler_params=pltpu.CompilerParams(vmem_limit_bytes=1024 * 1024),
     )(*[pltpu.with_memory_space_constraint(array, pltpu.VMEM) for array in held])
     return (

time: 69.6 us -> 65.6 us (0.943)
  Pallas kernels: 68.8 us -> 64.7 us
    pallas_call x1, Pallas kernels: 66.6 us -> 62.5 us  [on_device(): pl.pallas_call(kernel, out_shape=tuple((pltpu.VMEM(*shape) for shape in s...]
where the time goes in v5:
time: 65.6 us; the launch traced here: 65.5 us
  Pallas kernels  64.7 us (99%)
  between operations  0.8 us (1%)
    pallas_call x1, Pallas kernels, on_device(): pl.pallas_call(kernel, out_shape=tuple((pltpu.VMEM(*shape) for shape in s...  62.5 us
    pallas_call x1, Pallas kernels, on_device(): pl.pallas_call(write_out, out_shape=tuple((jax.ShapeDtypeStruct(*shape) f...  2.23 us

profile of v5, /device:TPU:1, one launch (start us, length us, event | category | flops | bytes accessed | tf_op | source)
XLA Modules:
  0.0 65.5 jit_solution(8935010321540475137)
XLA Ops:
  0.6 62.5 %shard_map.128 = (bf16[1536,1024]{1,0:T(8,128)(2,1)S(1)}, f32[256,1024]{1,0:T(8,128)S(1)}, f32[80,1024]{1,0:T(8,128)S(1)}, f32[1,1024]{1,0:T(1,128)S(1)}, f32[1,1024]{1,0:T(1,128)S(1)}) custom-call(bf16[1536,1024]{1,0:T(8,128)(2,1)} %bitcast.9, f32[1,1024]{1,0:T(1,128)} %bitcast.13, bf16[1024,1024]{1,0:T(8,128)(2,1)} %w1_hbm.1, f32[1,1024]{1,0:T(1,128)} %bitcast.14, ...), custom_call_target="tpu_custom_call" | custom-call | flops 10000000000 | bytes 9000000 | tf_op jit(solution)/shard_map/pallas_call | solution.py:607
  63.1 2.2 %shard_map.129 = (bf16[1536,1024]{1,0:T(8,128)(2,1)}, f32[256,1024]{1,0:T(8,128)}, f32[80,1024]{1,0:T(8,128)}, f32[1,1024]{1,0:T(1,128)}, f32[1,1024]{1,0:T(1,128)}) custom-call(bf16[1536,1024]{1,0:T(8,128)(2,1)S(1)} %get-tuple-element.15.refs_0_, f32[256,1024]{1,0:T(8,128)S(1)} %get-tuple-element.16.refs_1_, f32[80,1024]{1,0:T(8,128)S(1)} %get-tuple-element.17.refs_2_, ...), custom_call_target="tpu_custom_call" | custom-call | tf_op jit(solution)/shard_map/pallas_call | solution.py:628

commit v6 on v5

--- a/solution.py
+++ b/solution.py
@@ -121,7 +121,6 @@
 
     def normalise(i):
         rows = chunk_rows(i)
-        loads[i].wait()
         xf = x_ref[rows, :].astype(F32)
         inv = lax.rsqrt(jnp.mean(xf * xf, axis=-1, keepdims=True) + 1e-05)
         inv_ref[rows, :] = jnp.broadcast_to(inv, (CHUNK, LANES))
@@ -142,10 +141,13 @@
         onehot = jnp.concatenate([left.astype(F32), right.astype(F32)], axis=1).astype(BF16)
         s_ref[i * 16 : (i + 1) * 16, :] = jnp.dot(onehot, act, preferred_element_type=F32)
 
+    loads[0].wait()
     normalise(0)
     for copy in wloads:
         copy.wait()
     for i in range(NCHUNK):
+        if i + 1 < NCHUNK:
+            loads[i + 1].wait()
         first_dot(i)
         if i + 1 < NCHUNK:
             normalise(i + 1)
@@ -256,10 +258,10 @@
                     u_ref[rows, cols].astype(F32) * fb_ref[r : r + 1, :]
                 ).astype(BF16)
 
-    def hidden_tile(ref, slot, t):
-        tile = contract(n_ref[...], p_ref[slot])
+    def hidden_tile(ref, slot, t, part):
+        tile = contract(n_ref[:, part * 512 : (part + 1) * 512], p_ref[slot])
         for way in range(2):
-            ref[t, way] = tile[:, way * LANES : (way + 1) * LANES].reshape(NY, NX, 64, LANES)
+            ref[t, way, 2 * part : 2 * part + 2] = tile[:, way * LANES : (way + 1) * LANES].reshape(2, NX, 64, LANES)
 
     sibling = x * 2 + 1 - core
     tiles = ((give_ref, 1 - core, 0), (own_ref, core, 0), (give_ref, 1 - core, 1), (own_ref, core, 1))
@@ -290,7 +292,8 @@
         )
 
     def first(t):
-        to_core[t].wait_recv()
+        for part in range(2):
+            to_core[t, part].wait_recv()
         own_ref[t] = own_ref[t] + take_ref[t]
         for way in range(2):
             opposite = lax.rem(place(way) + 2, 4)
@@ -309,19 +312,26 @@
                 mid[...] = mid[...] + pass_ref[t, way, which]
                 hop(aggs, t, way, which, step, owner, agg_ref, 4 + which)
 
-    to_core = []
+    to_core = {}
     scale_tile(0, *tiles[0][1:])
     for slot in range(4):
         ref, _, t = tiles[slot]
-        hidden_tile(ref, slot, t)
-        if ref is give_ref:
-            to_core.append(
-                launch(remote(give_ref.at[t], take_ref.at[t], core_s.at[t], core_r.at[t], lon=sibling))
-            )
-        if slot < 3:
-            scale_tile(slot + 1, *tiles[slot + 1][1:])
+        for part in range(2):
+            hidden_tile(ref, slot, t, part)
+            if part == 0 and slot < 3:
+                scale_tile(slot + 1, *tiles[slot + 1][1:])
+            if ref is give_ref:
+                y_half = pl.ds(2 * part, 2)
+                to_core[t, part] = launch(
+                    remote(
+                        give_ref.at[t, :, y_half],
+                        take_ref.at[t, :, y_half],
+                        core_s.at[t, part],
+                        core_r.at[t, part],
+                        lon=sibling,
+                    )
+                )
         if slot == 2:
-            pass
             first(0)
     first(1)
 
@@ -591,7 +601,7 @@
         dma((7,)),
         dma((7,)), dma((7,)),
         dma((7,)), dma((7,)),
-        dma((2,)), dma((2,)),
+        dma((2, 2)), dma((2, 2)),
         dma((2, 2, 6)), dma((2, 2, 6)),
         dma((2, 2, 3)), dma((2, 2, 3)),
         dma((2, 7)), dma((2, 7)),

time: 65.6 us -> 64.7 us (0.986)
  Pallas kernels: 64.7 us -> 63.8 us
    pallas_call x1, Pallas kernels: 62.5 us -> 61.6 us  [on_device(): pl.pallas_call(kernel, out_shape=tuple((pltpu.VMEM(*shape) for shape in s...]
where the time goes in v6:
time: 64.7 us; the launch traced here: 64.6 us
  Pallas kernels  63.8 us (99%)
  between operations  0.8 us (1%)
    pallas_call x1, Pallas kernels, on_device(): pl.pallas_call(kernel, out_shape=tuple((pltpu.VMEM(*shape) for shape in s...  61.6 us
    pallas_call x1, Pallas kernels, on_device(): pl.pallas_call(write_out, out_shape=tuple((jax.ShapeDtypeStruct(*shape) f...  2.23 us

profile of v6, /device:TPU:1, one launch (start us, length us, event | category | flops | bytes accessed | tf_op | source)
XLA Modules:
  0.0 64.6 jit_solution(12178717529963529406)
XLA Ops:
  0.6 61.6 %shard_map.128 = (bf16[1536,1024]{1,0:T(8,128)(2,1)S(1)}, f32[256,1024]{1,0:T(8,128)S(1)}, f32[80,1024]{1,0:T(8,128)S(1)}, f32[1,1024]{1,0:T(1,128)S(1)}, f32[1,1024]{1,0:T(1,128)S(1)}) custom-call(bf16[1536,1024]{1,0:T(8,128)(2,1)} %bitcast.9, f32[1,1024]{1,0:T(1,128)} %bitcast.13, bf16[1024,1024]{1,0:T(8,128)(2,1)} %w1_hbm.1, f32[1,1024]{1,0:T(1,128)} %bitcast.14, ...), custom_call_target="tpu_custom_call" | custom-call | flops 10000000000 | bytes 9000000 | tf_op jit(solution)/shard_map/pallas_call | solution.py:617
  62.2 2.2 %shard_map.129 = (bf16[1536,1024]{1,0:T(8,128)(2,1)}, f32[256,1024]{1,0:T(8,128)}, f32[80,1024]{1,0:T(8,128)}, f32[1,1024]{1,0:T(1,128)}, f32[1,1024]{1,0:T(1,128)}) custom-call(bf16[1536,1024]{1,0:T(8,128)(2,1)S(1)} %get-tuple-element.15.refs_0_, f32[256,1024]{1,0:T(8,128)S(1)} %get-tuple-element.16.refs_1_, f32[80,1024]{1,0:T(8,128)S(1)} %get-tuple-element.17.refs_2_, ...), custom_call_target="tpu_custom_call" | custom-call | tf_op jit(solution)/shard_map/pallas_call | solution.py:638

commit v7 on v6

--- a/solution.py
+++ b/solution.py
@@ -353,6 +353,8 @@
 
     for i in range(NCHUNK):
         latent_grad(i)
+        if i == NCHUNK - 2:
+            ring(0)
 
     small = jnp.zeros((8, D), F32)
     bias_sum = jnp.zeros((1, D), F32)
@@ -448,9 +450,10 @@
             spot = hid_ref.at[core, t, lax.rem(x + 4 - k, NX), pl.ds(start, stop - start)]
             agc[t, g, k] = launch(remote(spot, spot, agc_s.at[t, g, k], agc_r.at[t, g, k], lon=sibling))
 
-    def place_rows(half, t):
+    def place_rows(half, t, g):
+        start, stop = groups[t][g]
         for xi in range(NX):
-            for k in range(NZ):
+            for k in (k for k in range(NZ) if start <= slot_of[k] < stop):
                 rows = pl.ds(pl.multiple_of(xi * 64 + lax.rem(z + k, NZ) * 8, 8), 8)
                 for way in range(2):
                     cols = pl.ds(pl.multiple_of(half * 512 + t * 256 + way * LANES, LANES), LANES)
@@ -461,7 +464,6 @@
             copy.wait_send()
         del sent[:count]
 
-    ring(0)
     ring(1)
     drain(len(ex1) + len(ex2) + len(to_core))
     cross(0)
@@ -511,20 +513,22 @@
     drain(len(agz) + len(sm4))
     to_sibling(0, 0)
     to_sibling(0, 1)
-    place_rows(core, 0)
+    for g in range(2):
+        place_rows(core, 0, g)
     to_sibling(1, 0)
     to_sibling(1, 1)
-    place_rows(core, 1)
     drain(len(agx))
     for g in range(2):
         for k in range(4):
             agc[0, g, k].wait_recv()
-    place_rows(1 - core, 0)
+        place_rows(1 - core, 0, g)
+    for g in range(2):
+        place_rows(core, 1, g)
     drain(len(sent))
     for g in range(2):
         for k in range(4):
             agc[1, g, k].wait_recv()
-    place_rows(1 - core, 1)
+        place_rows(1 - core, 1, g)
 
 
 def write_out(*refs):

time: 64.7 us -> 64.6 us (level)
  no operation moved by 1% of the time
where the time goes in v7:
time: 64.6 us; the launch traced here: 64.5 us
  Pallas kernels  63.7 us (99%)
  between operations  0.8 us (1%)
    pallas_call x1, Pallas kernels, on_device(): pl.pallas_call(kernel, out_shape=tuple((pltpu.VMEM(*shape) for shape in s...  61.5 us
    pallas_call x1, Pallas kernels, on_device(): pl.pallas_call(write_out, out_shape=tuple((jax.ShapeDtypeStruct(*shape) f...  2.23 us

profile of v7, /device:TPU:1, one launch (start us, length us, event | category | flops | bytes accessed | tf_op | source)
XLA Modules:
  0.0 64.5 jit_solution(2556431671168255919)
XLA Ops:
  0.6 61.5 %shard_map.128 = (bf16[1536,1024]{1,0:T(8,128)(2,1)S(1)}, f32[256,1024]{1,0:T(8,128)S(1)}, f32[80,1024]{1,0:T(8,128)S(1)}, f32[1,1024]{1,0:T(1,128)S(1)}, f32[1,1024]{1,0:T(1,128)S(1)}) custom-call(bf16[1536,1024]{1,0:T(8,128)(2,1)} %bitcast.9, f32[1,1024]{1,0:T(1,128)} %bitcast.13, bf16[1024,1024]{1,0:T(8,128)(2,1)} %w1_hbm.1, f32[1,1024]{1,0:T(1,128)} %bitcast.14, ...), custom_call_target="tpu_custom_call" | custom-call | flops 10000000000 | bytes 9000000 | tf_op jit(solution)/shard_map/pallas_call | solution.py:621
  62.1 2.2 %shard_map.129 = (bf16[1536,1024]{1,0:T(8,128)(2,1)}, f32[256,1024]{1,0:T(8,128)}, f32[80,1024]{1,0:T(8,128)}, f32[1,1024]{1,0:T(1,128)}, f32[1,1024]{1,0:T(1,128)}) custom-call(bf16[1536,1024]{1,0:T(8,128)(2,1)S(1)} %get-tuple-element.15.refs_0_, f32[256,1024]{1,0:T(8,128)S(1)} %get-tuple-element.16.refs_1_, f32[80,1024]{1,0:T(8,128)S(1)} %get-tuple-element.17.refs_2_, ...), custom_call_target="tpu_custom_call" | custom-call | tf_op jit(solution)/shard_map/pallas_call | solution.py:642

commit v8 on v7

--- a/solution.py
+++ b/solution.py
@@ -294,12 +294,19 @@
     def first(t):
         for part in range(2):
             to_core[t, part].wait_recv()
-        own_ref[t] = own_ref[t] + take_ref[t]
+        def add(way, step):
+            owner = lax.rem(place(way) + step, 4)
+            block = (t, way, owner) if way == 0 else (t, way, slice(None), owner)
+            own_ref[block] = own_ref[block] + take_ref[block]
+
         for way in range(2):
             opposite = lax.rem(place(way) + 2, 4)
+            add(way, 2)
             hop(passes, t, way, 0, 1, opposite, pass_ref, 0)
             hop(passes, t, way, 1, 3, opposite, pass_ref, 1)
         for way in range(2):
+            for step in (1, 3, 0):
+                add(way, step)
             hop(plains, t, way, 1, 1, lax.rem(place(way) + 1, 4), plain_ref, 2)
             hop(plains, t, way, 0, 3, lax.rem(place(way) + 3, 4), plain_ref, 3)
 

time: 64.6 us -> 64.3 us (level)
  no operation moved by 1% of the time
where the time goes in v8:
time: 64.3 us; the launch traced here: 64.2 us
  Pallas kernels  63.4 us (99%)
  between operations  0.8 us (1%)
    pallas_call x1, Pallas kernels, on_device(): pl.pallas_call(kernel, out_shape=tuple((pltpu.VMEM(*shape) for shape in s...  61.1 us
    pallas_call x1, Pallas kernels, on_device(): pl.pallas_call(write_out, out_shape=tuple((jax.ShapeDtypeStruct(*shape) f...  2.23 us

profile of v8, /device:TPU:1, one launch (start us, length us, event | category | flops | bytes accessed | tf_op | source)
XLA Modules:
  0.0 64.2 jit_solution(15383022072964703692)
XLA Ops:
  0.6 61.1 %shard_map.128 = (bf16[1536,1024]{1,0:T(8,128)(2,1)S(1)}, f32[256,1024]{1,0:T(8,128)S(1)}, f32[80,1024]{1,0:T(8,128)S(1)}, f32[1,1024]{1,0:T(1,128)S(1)}, f32[1,1024]{1,0:T(1,128)S(1)}) custom-call(bf16[1536,1024]{1,0:T(8,128)(2,1)} %bitcast.9, f32[1,1024]{1,0:T(1,128)} %bitcast.13, bf16[1024,1024]{1,0:T(8,128)(2,1)} %w1_hbm.1, f32[1,1024]{1,0:T(1,128)} %bitcast.14, ...), custom_call_target="tpu_custom_call" | custom-call | flops 10000000000 | bytes 9000000 | tf_op jit(solution)/shard_map/pallas_call | solution.py:628
  61.8 2.2 %shard_map.129 = (bf16[1536,1024]{1,0:T(8,128)(2,1)}, f32[256,1024]{1,0:T(8,128)}, f32[80,1024]{1,0:T(8,128)}, f32[1,1024]{1,0:T(1,128)}, f32[1,1024]{1,0:T(1,128)}) custom-call(bf16[1536,1024]{1,0:T(8,128)(2,1)S(1)} %get-tuple-element.15.refs_0_, f32[256,1024]{1,0:T(8,128)S(1)} %get-tuple-element.16.refs_1_, f32[80,1024]{1,0:T(8,128)S(1)} %get-tuple-element.17.refs_2_, ...), custom_call_target="tpu_custom_call" | custom-call | tf_op jit(solution)/shard_map/pallas_call | solution.py:649
